TPU v7x, 32 devices: a whole 2x2x4 slice. The times are simulated.
32 devices in a mesh: groups: 2 (over y), tensor: 8 (over z, x), dp: 2 (over core).
Axes of the slice: x: 2, y: 2, z: 4, core: 2. Of those that a mesh axis runs over, the one named last changes fastest.
Arguments:
- features: bfloat16 [4096, 1024], P('tensor', ('groups', 'dp')), parts along dimension 1, may hold values from -6 to 6
- table_up: int32 [4, 64], replicated, may hold values from 0 to 1
- table_down: int32 [4, 64], replicated, may hold values from 0 to 1
- w_up: bfloat16 [4, 256, 16384], P(None, None, 'tensor'), may hold values from -0.1875 to 0.1875
- u_up: bfloat16 [4096, 256], P('tensor'), may hold values from -0.09375 to 0.09375
- v_up: bfloat16 [16384, 256], P('tensor'), may hold values from -0.375 to 0.375
- w_down: bfloat16 [4, 256, 16384], P(None, None, 'tensor'), may hold values from -0.09375 to 0.09375
- u_down: bfloat16 [4096, 256], P('tensor'), may hold values from -0.375 to 0.375
- v_down: bfloat16 [16384, 256], P('tensor'), may hold values from -0.046875 to 0.046875
- cotangent: bfloat16 [4096, 1024], P('tensor', ('groups', 'dp')), parts along dimension 1, may hold values from -6 to 6
Outputs:
- output: bfloat16 [4096, 1024], P('tensor', ('groups', 'dp')), parts along dimension 1
- grad_features: bfloat16 [4096, 1024], P('tensor', ('groups', 'dp')), parts along dimension 1
- grad_w_up: float32 [8, 256, 16384], P('groups', 'dp', 'tensor'), parts along dimension 0
- grad_w_down: float32 [8, 256, 16384], P('groups', 'dp', 'tensor'), parts along dimension 0
- grad_u_up: float32 [8192, 256], P(('groups', 'tensor'), 'dp'), parts along dimension 0
- grad_v_up: float32 [32768, 256], P(('groups', 'tensor'), 'dp'), parts along dimension 0
- grad_u_down: float32 [8192, 256], P(('groups', 'tensor'), 'dp'), parts along dimension 0
- grad_v_down: float32 [32768, 256], P(('groups', 'tensor'), 'dp'), parts along dimension 0
There are 2 independent parts, one for each index of `groups`. A program takes and returns all parts, laid end to end along the dimension named above; an argument that names none is the same for every part. Nothing has to cross between parts.
Inputs may be any that keep to these rules, and one draw needn't show every extreme that they name: `table_up`: each entry names one block of 256 features within a panel of 512 features. `table_down`: each entry names one block of 256 features within a panel of 512 features.
All inputs are finite; a program needn't handle non-finite values.
Results may differ from a plain program's by a relative error of at most 0.006.
Values may be sent and summed in bfloat16 or wider, within the bound.
A program may use at most 192 MiB of HBM per device.

v0:
```python
import math

import jax
import jax.numpy as jnp
from jax import lax
from jax.sharding import PartitionSpec as P

root_half = 1.0 / math.sqrt(2.0)
inv_root_tau = 1.0 / math.sqrt(2.0 * math.pi)


def from_partner(array, axis, distance):
    return lax.ppermute(array, axis, [(i, i ^ 1 << distance) for i in range(lax.axis_size(axis))])


def gelu_value(values):
    return 0.5 * values * (1.0 + lax.erf(values * root_half))


def gelu_slope(values):
    return (
        0.5 * (1.0 + lax.erf(values * root_half))
        + values * jnp.exp(-0.5 * values * values) * inv_root_tau
    )


def panel_trade(values, bit_index):
    return from_partner(values, "tensor", bit_index)


def partial_trade(values, bit_index):
    return from_partner(values, "tensor", bit_index)


def block_ids(device, geometry):
    block_rows, hidden, column_width, block_count = (
        geometry[3],
        geometry[4],
        geometry[5],
        geometry[6],
    )
    starts = device * hidden + jnp.arange(block_count, dtype=jnp.int32) * column_width
    return starts // block_rows


def lookup(selector, slot_index, device, geometry):
    return jnp.take(selector[slot_index], block_ids(device, geometry), axis=0)


def pick_blocks(panel_rows, chosen, block_rows):
    stacked = panel_rows.reshape(panel_rows.shape[0] // block_rows, block_rows, panel_rows.shape[1])
    return jnp.take(stacked, chosen, axis=0)


def place_blocks(portion, chosen, block_rows, panel_size):
    per_panel = panel_size // block_rows
    onehot = (chosen[:, None] == jnp.arange(per_panel, dtype=jnp.int32)[None, :]).astype(
        jnp.float32
    )
    placed = jnp.einsum("bn,brt->nrt", onehot, portion, precision=lax.Precision.HIGHEST)
    return placed.reshape(panel_size, portion.shape[2])


def group_gather(portion, axis_dim, group_bits, device):
    for bit_index in range(group_bits):
        partner_rows = panel_trade(portion, bit_index)
        is_upper = device >> bit_index & 1 == 1
        portion = jnp.where(
            is_upper,
            jnp.concatenate([partner_rows, portion], axis=axis_dim),
            jnp.concatenate([portion, partner_rows], axis=axis_dim),
        )
    return portion


def fetch_blocks(shard_rows, selector, geometry):
    device, group_bits, levels, block_rows = (geometry[0], geometry[1], geometry[2], geometry[3])
    own_panel = group_gather(shard_rows, 0, group_bits, device)
    selected = [pick_blocks(own_panel, lookup(selector, 0, device, geometry), block_rows)]
    for level_index in range(levels):
        bit_index = group_bits + level_index
        partner = device ^ 1 << bit_index
        wanted = pick_blocks(
            own_panel, lookup(selector, level_index + 1, partner, geometry), block_rows
        )
        selected.append(panel_trade(wanted, bit_index))
    return jnp.stack(selected)


def reduce_partials(contrib, selector, geometry):
    device, group_bits, levels, block_rows, panel_size = (
        geometry[0],
        geometry[1],
        geometry[2],
        geometry[3],
        geometry[7],
    )
    summed = place_blocks(contrib[0], lookup(selector, 0, device, geometry), block_rows, panel_size)
    for level_index in range(levels):
        bit_index = group_bits + level_index
        partner = device ^ 1 << bit_index
        arrived = partial_trade(contrib[level_index + 1], bit_index)
        summed = summed + place_blocks(
            arrived, lookup(selector, level_index + 1, partner, geometry), block_rows, panel_size
        )
    for bit_index in reversed(range(group_bits)):
        half_rows = summed.shape[0] // 2
        is_upper = device >> bit_index & 1 == 1
        kept_rows = jnp.where(is_upper, summed[half_rows:], summed[:half_rows])
        sent_rows = jnp.where(is_upper, summed[:half_rows], summed[half_rows:])
        summed = kept_rows + partial_trade(sent_rows, bit_index)
    return summed


def on_device(features, table_up, table_down, w_up, u_up, v_up, w_down, u_down, v_down, cotangent):
    device = lax.axis_index("tensor")
    slot_count, block_rows, hidden = w_up.shape
    levels = slot_count - 1
    group_bits = lax.axis_size("tensor").bit_length() - 1 - levels
    column_width = min(block_rows, hidden)
    block_count = hidden // column_width
    tokens_here = features.shape[1]
    panel_size = features.shape[0] * (1 << group_bits)
    geometry = (
        device,
        group_bits,
        levels,
        block_rows,
        hidden,
        column_width,
        block_count,
        panel_size,
    )
    up_blocks = w_up.reshape(slot_count, block_rows, block_count, column_width)
    down_blocks = w_down.reshape(slot_count, block_rows, block_count, column_width)
    a_up = lax.psum(jnp.dot(u_up.T, features, preferred_element_type=jnp.float32), "tensor")
    a_up_b = a_up.astype(jnp.bfloat16)
    picked_features = fetch_blocks(features, table_up, geometry)
    preact = jnp.einsum(
        "srbw,sbrt->bwt", up_blocks, picked_features, preferred_element_type=jnp.float32
    ).reshape(hidden, tokens_here)
    preact = preact + jnp.dot(v_up, a_up_b, preferred_element_type=jnp.float32)
    activation = gelu_value(preact).astype(jnp.bfloat16)
    a_down = lax.psum(jnp.dot(v_down.T, activation, preferred_element_type=jnp.float32), "tensor")
    a_down_b = a_down.astype(jnp.bfloat16)
    act_blocks = activation.reshape(block_count, column_width, tokens_here)
    partial_out = jnp.einsum(
        "srbw,bwt->sbrt", down_blocks, act_blocks, preferred_element_type=jnp.float32
    )
    output = (
        reduce_partials(partial_out, table_down, geometry)
        + jnp.dot(u_down, a_down_b, preferred_element_type=jnp.float32)
    ).astype(jnp.bfloat16)
    b_down = lax.psum(jnp.dot(u_down.T, cotangent, preferred_element_type=jnp.float32), "tensor")
    b_down_b = b_down.astype(jnp.bfloat16)
    picked_cotangent = fetch_blocks(cotangent, table_down, geometry)
    grad_act = jnp.einsum(
        "srbw,sbrt->bwt", down_blocks, picked_cotangent, preferred_element_type=jnp.float32
    ).reshape(hidden, tokens_here)
    grad_act = grad_act + jnp.dot(v_down, b_down_b, preferred_element_type=jnp.float32)
    grad_pre = (grad_act * gelu_slope(preact)).astype(jnp.bfloat16)
    grad_w_down = jnp.einsum(
        "sbrt,bwt->srbw", picked_cotangent, act_blocks, preferred_element_type=jnp.float32
    ).reshape(slot_count, block_rows, hidden)
    grad_u_down = jnp.dot(cotangent, a_down_b.T, preferred_element_type=jnp.float32)
    grad_v_down = jnp.dot(activation, b_down_b.T, preferred_element_type=jnp.float32)
    grad_w_down, grad_u_down, grad_v_down = (
        lax.psum_scatter(grad_w_down, "dp", scatter_dimension=1, tiled=True),
        lax.psum_scatter(grad_u_down, "dp", scatter_dimension=1, tiled=True),
        lax.psum_scatter(grad_v_down, "dp", scatter_dimension=1, tiled=True),
    )
    b_up = lax.psum(jnp.dot(v_up.T, grad_pre, preferred_element_type=jnp.float32), "tensor")
    b_up_b = b_up.astype(jnp.bfloat16)
    pre_blocks = grad_pre.reshape(block_count, column_width, tokens_here)
    partial_back = jnp.einsum(
        "srbw,bwt->sbrt", up_blocks, pre_blocks, preferred_element_type=jnp.float32
    )
    grad_features = (
        reduce_partials(partial_back, table_up, geometry)
        + jnp.dot(u_up, b_up_b, preferred_element_type=jnp.float32)
    ).astype(jnp.bfloat16)
    grad_w_up = jnp.einsum(
        "sbrt,bwt->srbw", picked_features, pre_blocks, preferred_element_type=jnp.float32
    ).reshape(slot_count, block_rows, hidden)
    grad_u_up = jnp.dot(features, b_up_b.T, preferred_element_type=jnp.float32)
    grad_v_up = jnp.dot(grad_pre, a_up_b.T, preferred_element_type=jnp.float32)
    grad_w_up, grad_u_up, grad_v_up = (
        lax.psum_scatter(grad_w_up, "dp", scatter_dimension=1, tiled=True),
        lax.psum_scatter(grad_u_up, "dp", scatter_dimension=1, tiled=True),
        lax.psum_scatter(grad_v_up, "dp", scatter_dimension=1, tiled=True),
    )
    return (
        output,
        grad_features,
        grad_w_up,
        grad_w_down,
        grad_u_up,
        grad_v_up,
        grad_u_down,
        grad_v_down,
    )


def solution(mesh):
    return jax.shard_map(
        on_device,
        mesh=mesh,
        in_specs=(
            P("tensor", ("groups", "dp")),
            P(),
            P(),
            P(None, None, "tensor"),
            P("tensor", None),
            P("tensor", None),
            P(None, None, "tensor"),
            P("tensor", None),
            P("tensor", None),
            P("tensor", ("groups", "dp")),
        ),
        out_specs=(
            P("tensor", ("groups", "dp")),
            P("tensor", ("groups", "dp")),
            P("groups", "dp", "tensor"),
            P("groups", "dp", "tensor"),
            P(("groups", "tensor"), "dp"),
            P(("groups", "tensor"), "dp"),
            P(("groups", "tensor"), "dp"),
            P(("groups", "tensor"), "dp"),
        ),
        check_vma=False,
    )
```

profile of v0, /device:TPU:0, one launch (start us, length us, event | category | flops | bytes accessed | tf_op | source)
XLA Modules:
  0.0 466.7 jit_solution(2810248760847787796)
XLA Ops:
  10.3 1.6 gather_fusion.15
  13.0 4.0 collective-permute-start.8
  19.1 1.1 broadcast_select_fusion.1
  20.2 1.6 collective-permute-start.7
  23.2 1.6 gather_fusion.13
  24.7 2.4 broadcast_select_fusion.2
  27.1 1.5 collective-permute-start.6
  28.6 1.6 gather_fusion.8
  30.2 2.4 broadcast_select_fusion.3
  32.9 1.6 gather_fusion.6
  34.5 2.4 broadcast_select_fusion.4
  40.0 1.6 gather_fusion.4
  41.6 1.2 select_bitcast_fusion
  43.2 1.2 broadcast_select_fusion.5
  44.3 5.7 %copy.87 = bf16[128,8,8,256]{3,2,1,0:T(8,128)(2,1)} copy(bf16[128,8,8,256]{3,1,2,0:T(8,128)(2,1)} %bitcast.185) | data formatting | bytes 8388608
  50.0 7.5 %copy.50 = bf16[4,256,8,256]{1,3,0,2:T(8,128)(2,1)} copy(bf16[4,256,8,256]{3,2,1,0:T(8,128)(2,1)} %bitcast.184) | data formatting | bytes 8388608 | tf_op jit(solution)/shard_map/reshape | solution.py:135
  57.5 1.6 gather_fusion.2
  59.1 86.1 %all-reduce.4 = (bf16[256,256]{1,0:T(8,128)(2,1)S(1)}, bf16[256,256]{1,0:T(8,128)(2,1)S(1)}) all-reduce(f32[256,256]{1,0:T(8,128)S(1)} %fusion.68, f32[256,256]{1,0:T(8,128)S(1)} %fusion.69), channel_id=1, replica_groups=mesh['groups'=2,'tensor'=8,'dp'=2] {'tensor'}, use_global_device_ids=true, to_apply=%region_0.3 | all-reduce | flops 131072 | bytes 786432 | tf_op jit(solution)/shard_map/psum | solution.py:136
  145.2 1.8 convolution_bitcast_fusion.3
  147.0 1.9 convolution_bitcast_fusion.4
  149.1 1.5 copy-done.4
  150.7 4.5 fusion.17
  155.1 2.9 copy.78
  158.0 9.5 %collective-permute-done = bf16[8,256,256]{2,1,0:T(8,128)(2,1)} collective-permute-done((bf16[8,256,256]{2,1,0:T(8,128)(2,1)}, bf16[8,256,256]{2,1,0:T(8,128)(2,1)}, u32[]{:S(2)}, u32[]{:S(2)}) %collective-permute-start) | collective-permute-done | bytes 1048608 | tf_op jit(solution)/shard_map/ppermute | solution.py:13
  167.6 5.8 %fusion = f32[8,256,256,1]{1,2,3,0:T(8,128)} fusion(bf16[4,32,8,8,256]{4,3,2,1,0:T(8,128)(2,1)} %bitcast.186, bf16[1,8,256,256]{3,2,0,1:T(8,128)(2,1)} %bitcast.10, bf16[1,8,256,256]{3,2,0,1:T(8,128)(2,1)} %bitcast.8, bf16[1,8,256,256]{3,2,0,1:T(8,128)(2,1)} %bitcast.6, bf16[1,8,256,256]{3,2,0,1:T(8,128)(2,1)S(1)} %select_bitcast_fusion.1), kind=kOutput, calls=%fused_computation.16 | convolution fusion | flops 1090519040 | bytes 10485760 | tf_op jit(solution)/shard_map/srbw,sbrt->bwt/dot_general | solution.py:139
  173.4 3.0 copy.41
  176.3 4.0 fusion.14
  182.4 40.1 %all-reduce.5 = (bf16[256,256]{0,1:T(8,128)(2,1)S(1)}, bf16[256,256]{0,1:T(8,128)(2,1)S(1)}) all-reduce(f32[256,256]{0,1:T(8,128)S(1)} %convolution_bitcast_fusion.10, f32[256,256]{0,1:T(8,128)S(1)} %convolution_bitcast_fusion.9), channel_id=1, replica_groups=mesh['groups'=2,'tensor'=8,'dp'=2] {'tensor'}, use_global_device_ids=true, to_apply=%region_1.0 | all-reduce | flops 131072 | bytes 786432 | tf_op jit(solution)/shard_map/psum | solution.py:144
  225.7 1.6 copy.74
  227.3 3.5 convolution_bitcast_fusion.1
  230.8 3.9 copy.61
  234.7 1.3 copy.86
  236.0 1.6 copy.75
  237.6 3.1 convolution_bitcast_fusion
  240.7 3.8 copy.63
  245.5 1.8 fusion.71
  247.3 3.5 convolution_bitcast_fusion.2
  250.8 4.2 slice_bitcast_fusion.5
  255.0 2.5 collective-permute-start.4
  257.5 1.9 fusion.70
  259.5 4.0 fusion.6
  263.5 3.5 slice_bitcast_fusion.1
  267.9 2.0 collective-permute-start.9
  269.9 77.3 %collective-permute-done.5 = f32[8,256,256]{1,2,0:T(8,128)} collective-permute-done((f32[8,256,256]{1,2,0:T(8,128)}, f32[8,256,256]{1,2,0:T(8,128)}, u32[]{:S(2)}, u32[]{:S(2)}) %collective-permute-start.5) | collective-permute-done | bytes 2097184 | tf_op jit(solution)/shard_map/ppermute | solution.py:13
  347.8 2.4 copy.44
  350.2 3.1 copy.54
  353.5 2.6 fusion.38
  356.2 1.9 fusion.32
  358.1 1.8 copy.68
  359.8 1.8 copy.69
  361.6 2.2 copy.47
  363.8 3.0 copy.45
  366.9 3.0 copy.46
  371.6 1.2 convolution_add_fusion.3
  373.2 1.4 fusion.16
  375.8 46.7 %collective-permute-done.11 = f32[8,256,256]{1,2,0:T(8,128)} collective-permute-done((f32[8,256,256]{1,2,0:T(8,128)}, f32[8,256,256]{1,2,0:T(8,128)}, u32[]{:S(2)}, u32[]{:S(2)}) %collective-permute-start.11) | collective-permute-done | bytes 2097184 | tf_op jit(solution)/shard_map/ppermute | solution.py:13
  422.5 2.2 copy.57
  424.7 3.0 copy.55
  427.8 11.9 %collective-permute-done.10 = f32[8,256,256]{1,2,0:T(8,128)} collective-permute-done((f32[8,256,256]{1,2,0:T(8,128)}, f32[8,256,256]{1,2,0:T(8,128)}, u32[]{:S(2)}, u32[]{:S(2)}) %collective-permute-start.10) | collective-permute-done | bytes 2097184 | tf_op jit(solution)/shard_map/ppermute | solution.py:13
  439.7 3.2 copy.56
  444.6 1.1 convolution_add_fusion.1
  446.2 1.4 fusion.15
  448.8 5.3 %copy.66 = f32[4,128,2048]{2,1,0:T(8,128)} copy(f32[4,128,2048]{1,2,0:T(8,128)} %reduce-scatter.7.cloned.1.call-done) | data formatting | bytes 8388608
  454.1 5.4 %copy.67 = f32[4,128,2048]{2,1,0:T(8,128)} copy(f32[4,128,2048]{1,2,0:T(8,128)} %reduce-scatter.9.cloned.1.call-done) | data formatting | bytes 8388608
  (173 shorter events, 25.7 us)
Async XLA Ops:
  7.2 138.0 %copy-start = (bf16[2048,256]{1,0:T(8,128)(2,1)S(1)}, bf16[2048,256]{1,0:T(8,128)(2,1)}, u32[]{:S(2)}) copy-start(bf16[2048,256]{1,0:T(8,128)(2,1)} %param.22) | copy-start | bytes 3145732
  7.2 350.9 %reduce-scatter.11.cloned.1.call-start = ((), (), s32[]{:S(2)}) async-start(), calls=%async_computation.8 | async-start | bytes 786432 | tf_op jit(solution)/shard_map/reduce_scatter | solution.py:189
  11.8 6.6 %copy-start.3 = (bf16[512,256]{1,0:T(8,128)(2,1)S(1)}, bf16[512,256]{1,0:T(8,128)(2,1)}, u32[]{:S(2)}) copy-start(bf16[512,256]{1,0:T(8,128)(2,1)} %param.23) | copy-start | bytes 786436
  13.0 135.9 %collective-permute-start.8 = (bf16[8,256,256]{2,1,0:T(8,128)(2,1)}, bf16[8,256,256]{2,1,0:T(8,128)(2,1)}, u32[]{:S(2)}, u32[]{:S(2)}) collective-permute-start(bf16[8,256,256]{2,1,0:T(8,128)(2,1)} %broadcast_select_fusion), channel_id=1, source_target_pairs={{0,8},{2,10},{4,12},{6,14},{8,0},{10,2},{12,4},{14,6},{1,9},{3,11}... | collective-permute-start | bytes 3145736 | tf_op jit(solution)/shard_map/ppermute | solution.py:13
  18.4 1.8 copy-start.38
  18.4 14.5 %copy-start.36 = (s32[8]{0:T(128)}, s32[8]{0:T(128)S(1)}, u32[]{:S(2)}) copy-start(s32[8]{0:T(128)S(1)} %get-tuple-element.67) | copy-start | bytes 100
  20.2 128.9 %collective-permute-start.7 = (bf16[8,256,256]{2,1,0:T(8,128)(2,1)}, bf16[8,256,256]{2,1,0:T(8,128)(2,1)}, u32[]{:S(2)}, u32[]{:S(2)}) collective-permute-start(bf16[8,256,256]{2,1,0:T(8,128)(2,1)} %broadcast_select_fusion.1), channel_id=1, source_target_pairs={{0,4},{2,6},{4,0},{6,2},{8,12},{10,14},{12,8},{14,10},{1,5},{3,7},... | collective-permute-start | bytes 3145736 | tf_op jit(solution)/shard_map/ppermute | solution.py:13
  23.1 4.0 copy-start.31
  23.1 5.5 %copy-start.2 = (bf16[512,256]{1,0:T(8,128)(2,1)S(1)}, bf16[512,256]{1,0:T(8,128)(2,1)}, u32[]{:S(2)}) copy-start(bf16[512,256]{1,0:T(8,128)(2,1)} %param.14) | copy-start | bytes 786436
  27.1 122.0 %collective-permute-start.6 = (bf16[8,256,256]{2,1,0:T(8,128)(2,1)}, bf16[8,256,256]{2,1,0:T(8,128)(2,1)}, u32[]{:S(2)}, u32[]{:S(2)}) collective-permute-start(bf16[8,256,256]{2,1,0:T(8,128)(2,1)} %broadcast_select_fusion.2), channel_id=1, source_target_pairs={{0,2},{2,0},{4,6},{6,4},{8,10},{10,8},{12,14},{14,12},{1,3},{3,1},... | collective-permute-start | bytes 3145736 | tf_op jit(solution)/shard_map/ppermute | solution.py:13
  32.6 125.4 %collective-permute-start.2 = (bf16[8,256,256]{2,1,0:T(8,128)(2,1)}, bf16[8,256,256]{2,1,0:T(8,128)(2,1)}, u32[]{:S(2)}, u32[]{:S(2)}) collective-permute-start(bf16[8,256,256]{2,1,0:T(8,128)(2,1)} %broadcast_select_fusion.3), channel_id=1, source_target_pairs={{0,8},{2,10},{4,12},{6,14},{8,0},{10,2},{12,4},{14,6},{1,9},{3,11}... | collective-permute-start | bytes 3145736 | tf_op jit(solution)/shard_map/ppermute | solution.py:13
  37.0 2.5 copy-start.21
  37.0 2.7 copy-start.19
  37.0 121.1 %collective-permute-start.1 = (bf16[8,256,256]{2,1,0:T(8,128)(2,1)}, bf16[8,256,256]{2,1,0:T(8,128)(2,1)}, u32[]{:S(2)}, u32[]{:S(2)}) collective-permute-start(bf16[8,256,256]{2,1,0:T(8,128)(2,1)} %broadcast_select_fusion.4), channel_id=1, source_target_pairs={{0,4},{2,6},{4,0},{6,2},{8,12},{10,14},{12,8},{14,10},{1,5},{3,7},... | collective-permute-start | bytes 3145736 | tf_op jit(solution)/shard_map/ppermute | solution.py:13
  38.8 2.8 copy-start.35
  38.8 5.6 %copy-start.33 = (s32[8]{0:T(128)}, s32[8]{0:T(128)S(1)}, u32[]{:S(2)}) copy-start(s32[8]{0:T(128)S(1)} %get-tuple-element.71) | copy-start | bytes 100
  41.6 1.6 copy-start.15
  59.1 88.0 %copy-start.12 = (bf16[2048,256]{1,0:T(8,128)(2,1)S(1)}, bf16[2048,256]{1,0:T(8,128)(2,1)}, u32[]{:S(2)}) copy-start(bf16[2048,256]{1,0:T(8,128)(2,1)} %param.19) | copy-start | bytes 3145732
  145.1 3.7 copy-start.29
  145.2 3.9 copy-start.23
  147.0 1.9 copy-start.14
  147.0 3.6 copy-start.4
  148.9 18.7 %collective-permute-start = (bf16[8,256,256]{2,1,0:T(8,128)(2,1)}, bf16[8,256,256]{2,1,0:T(8,128)(2,1)}, u32[]{:S(2)}, u32[]{:S(2)}) collective-permute-start(bf16[8,256,256]{2,1,0:T(8,128)(2,1)} %broadcast_select_fusion.5), channel_id=1, source_target_pairs={{0,2},{2,0},{4,6},{6,4},{8,10},{10,8},{12,14},{14,12},{1,3},{3,1},... | collective-permute-start | bytes 3145736 | tf_op jit(solution)/shard_map/ppermute | solution.py:13
  149.1 18.5 %copy-start.24 = (bf16[1,8,256,256]{3,2,0,1:T(8,128)(2,1)}, bf16[1,8,256,256]{3,2,0,1:T(8,128)(2,1)S(1)}, u32[]{:S(2)}) copy-start(bf16[1,8,256,256]{3,2,0,1:T(8,128)(2,1)S(1)} %select_bitcast_fusion.1) | copy-start | bytes 3145732
  180.4 1.0 copy-start.5
  180.4 1.6 copy-start.13
  182.4 43.0 %copy-start.6 = (bf16[2048,256]{0,1:T(8,128)(2,1)S(1)}, bf16[2048,256]{0,1:T(8,128)(2,1)}, u32[]{:S(2)}) copy-start(bf16[2048,256]{0,1:T(8,128)(2,1)} %copy-done.5) | copy-start | bytes 3145732
  222.6 2.8 copy-start.25
  222.6 2.8 copy-start.27
  223.7 136.1 %reduce-scatter.15.cloned.1.call-start = ((), (), s32[]{:S(2)}) async-start(), calls=%async_computation.10 | async-start | bytes 786432 | tf_op jit(solution)/shard_map/reduce_scatter | solution.py:169
  224.8 223.9 %reduce-scatter.7.cloned.1.call-start = ((), (), s32[]{:S(2)}) async-start(), calls=%async_computation.6 | async-start | bytes 12582912 | tf_op jit(solution)/shard_map/reduce_scatter | solution.py:188
  234.7 219.4 %reduce-scatter.9.cloned.1.call-start = ((), (), s32[]{:S(2)}) async-start(), calls=%async_computation.7 | async-start | bytes 12582912 | tf_op jit(solution)/shard_map/reduce_scatter | solution.py:168
  244.6 0.9 copy-start.30
  244.6 215.0 %reduce-scatter.13.cloned.1.call-start = ((), (), s32[]{:S(2)}) async-start(), calls=%async_computation.9 | async-start | bytes 3145728 | tf_op jit(solution)/shard_map/reduce_scatter | solution.py:190
  247.3 212.3 %reduce-scatter.17.cloned.1.call-start = ((), (), s32[]{:S(2)}) async-start(), calls=%async_computation.11 | async-start | bytes 3145728 | tf_op jit(solution)/shard_map/reduce_scatter | solution.py:170
  255.0 92.2 %collective-permute-start.5 = (f32[8,256,256]{1,2,0:T(8,128)}, f32[8,256,256]{1,2,0:T(8,128)}, u32[]{:S(2)}, u32[]{:S(2)}) collective-permute-start(f32[8,256,256]{1,2,0:T(8,128)} %get-tuple-element.51), channel_id=1, source_target_pairs={{0,8},{2,10},{4,12},{6,14},{8,0},{10,2},{12,4},{14,6},{1,9},{3,11}... | collective-permute-start | bytes 6291464 | tf_op jit(solution)/shard_map/ppermute | solution.py:13
  255.0 108.8 %collective-permute-start.3 = (f32[8,256,256]{1,2,0:T(8,128)}, f32[8,256,256]{1,2,0:T(8,128)}, u32[]{:S(2)}, u32[]{:S(2)}) collective-permute-start(f32[8,256,256]{1,2,0:T(8,128)} %get-tuple-element.52), channel_id=1, source_target_pairs={{0,2},{2,0},{4,6},{6,4},{8,10},{10,8},{12,14},{14,12},{1,3},{3,1},... | collective-permute-start | bytes 6291464 | tf_op jit(solution)/shard_map/ppermute | solution.py:13
  255.0 4.5 copy-start.16
  255.0 111.9 %collective-permute-start.4 = (f32[8,256,256]{1,2,0:T(8,128)}, f32[8,256,256]{1,2,0:T(8,128)}, u32[]{:S(2)}, u32[]{:S(2)}) collective-permute-start(f32[8,256,256]{1,2,0:T(8,128)} %get-tuple-element.50), channel_id=1, source_target_pairs={{0,4},{2,6},{4,0},{6,2},{8,12},{10,14},{12,8},{14,10},{1,5},{3,7},... | collective-permute-start | bytes 6291464 | tf_op jit(solution)/shard_map/ppermute | solution.py:13
  263.5 84.0 %copy-start.20 = (bf16[512,256]{1,0:T(8,128)(2,1)S(1)}, bf16[512,256]{1,0:T(8,128)(2,1)}, u32[]{:S(2)}) copy-start(bf16[512,256]{1,0:T(8,128)(2,1)} %param.21) | copy-start | bytes 786436
  263.5 84.0 %copy-start.28 = (bf16[256,256]{0,1:T(8,128)(2,1)S(1)}, bf16[256,256]{0,1:T(8,128)(2,1)}, u32[]{:S(2)}) copy-start(bf16[256,256]{0,1:T(8,128)(2,1)} %copy-done.27) | copy-start | bytes 393220
  267.0 155.5 %collective-permute-start.11 = (f32[8,256,256]{1,2,0:T(8,128)}, f32[8,256,256]{1,2,0:T(8,128)}, u32[]{:S(2)}, u32[]{:S(2)}) collective-permute-start(f32[8,256,256]{1,2,0:T(8,128)} %get-tuple-element.47), channel_id=1, source_target_pairs={{0,8},{2,10},{4,12},{6,14},{8,0},{10,2},{12,4},{14,6},{1,9},{3,11}... | collective-permute-start | bytes 6291464 | tf_op jit(solution)/shard_map/ppermute | solution.py:13
  267.9 156.8 %collective-permute-start.9 = (f32[8,256,256]{1,2,0:T(8,128)}, f32[8,256,256]{1,2,0:T(8,128)}, u32[]{:S(2)}, u32[]{:S(2)}) collective-permute-start(f32[8,256,256]{1,2,0:T(8,128)} %get-tuple-element.48), channel_id=1, source_target_pairs={{0,2},{2,0},{4,6},{6,4},{8,10},{10,8},{12,14},{14,12},{1,3},{3,1},... | collective-permute-start | bytes 6291464 | tf_op jit(solution)/shard_map/ppermute | solution.py:13
  347.2 92.5 %collective-permute-start.10 = (f32[8,256,256]{1,2,0:T(8,128)}, f32[8,256,256]{1,2,0:T(8,128)}, u32[]{:S(2)}, u32[]{:S(2)}) collective-permute-start(f32[8,256,256]{1,2,0:T(8,128)} %get-tuple-element.46), channel_id=1, source_target_pairs={{0,4},{2,6},{4,0},{6,2},{8,12},{10,14},{12,8},{14,10},{1,5},{3,7},... | collective-permute-start | bytes 6291464 | tf_op jit(solution)/shard_map/ppermute | solution.py:13
  350.2 3.1 copy-start.22
  350.2 3.1 copy-start.26
  353.3 2.9 copy-start.11
  353.3 2.9 copy-start.34
  369.9 1.6 copy-start.7
  369.9 1.7 copy-start.18
  369.9 1.7 copy-start.32
  371.6 1.6 copy-start.9
  371.6 1.6 copy-start.39
  442.9 1.6 copy-start.8
  442.9 1.7 copy-start.17
  444.6 1.6 copy-start.10
  444.6 1.6 copy-start.37
  454.1 5.4 %copy-start.1 = (bf16[2048,256]{1,0:T(8,128)(2,1)S(1)}, bf16[2048,256]{1,0:T(8,128)(2,1)}, u32[]{:S(2)}) copy-start(bf16[2048,256]{1,0:T(8,128)(2,1)} %param.22) | copy-start | bytes 3145732
Sparse Core Ops, SparseCore 0:
  223.8 6.9 reduce-scatter.10
  233.1 9.1 reduce-scatter.14
  244.6 17.9 reduce-scatter.6
  264.8 18.0 reduce-scatter.8
  285.6 10.8 reduce-scatter.12
  299.2 10.7 reduce-scatter.16
where the time goes:
time: 476 us; the launch traced here: 467 us
  waiting for transfers between devices  146 us (31%)
  blocking collectives  126 us (26%)
  local copies, waits for them, and re-layouts  101 us (21%)
  matrix products  47.6 us (10%)
  other arithmetic  16.4 us (3%)
  between operations  15.1 us (3%)
  starting transfers between devices  14.3 us (3%)
    ppermute x12, waiting for transfers between devices, from_partner(): lax.ppermute(array, axis, [(i, i ^ 1 << distance) for i in range(lax.axis...  146 us
    psum x1, blocking collectives, on_device(): lax.psum(jnp.dot(u_up.T, features, preferred_element_type=jnp.float32), '...  86.1 us
    psum x1, blocking collectives, on_device(): lax.psum(jnp.dot(v_down.T, activation, preferred_element_type=jnp.float32...  40.1 us
    unnamed x89, local copies, waits for them, and re-layouts  29.3 us
    ppermute x6, local copies, waits for them, and re-layouts, from_partner(): lax.ppermute(array, axis, [(i, i ^ 1 << distance) for i in range(lax.axis...  16.7 us
    ppermute x12, starting transfers between devices, from_partner(): lax.ppermute(array, axis, [(i, i ^ 1 << distance) for i in range(lax.axis...  13.6 us
    dot_general x8, matrix products, place_blocks(): jnp.einsum('bn,brt->nrt', onehot, portion, precision=lax.Precision.HIGHEST)  11.8 us
    gather x8, local copies, waits for them, and re-layouts, pick_blocks(): return jnp.take(stacked, chosen, axis=0)  10.7 us
  transfers between devices with their start and end apart: 18, of which 4 were waited for; matrix products, arithmetic and copies ran while one was open for 30% of the time, Pallas kernels for 0%

commit v1 on v0

--- a/solution.py
+++ b/solution.py
@@ -1,8 +1,11 @@
+import functools
 import math
 
 import jax
 import jax.numpy as jnp
 from jax import lax
+from jax.experimental import pallas as pl
+from jax.experimental.pallas import tpu as pltpu
 from jax.sharding import PartitionSpec as P
 
 root_half = 1.0 / math.sqrt(2.0)
@@ -201,9 +204,496 @@
     )
 
 
+F32, BF16 = jnp.float32, jnp.bfloat16
+VMEM_BYTES = 56 * 2**20
+
+
+def nn(a, b):
+    return lax.dot_general(a, b, (((1,), (0,)), ((), ())), preferred_element_type=F32)
+
+
+def nt(a, b):
+    return lax.dot_general(a, b, (((1,), (1,)), ((), ())), preferred_element_type=F32)
+
+
+def tn(a, b):
+    return lax.dot_general(a, b, (((0,), (0,)), ((), ())), preferred_element_type=F32)
+
+
+def flip(me, offset):
+    peer = me
+    for k in range(offset.bit_length()):
+        if offset >> k & 1:
+            peer = peer + (1 << k) * (1 - 2 * ((me // (1 << k)) % 2))
+    return peer
+
+
+def remote(src, dst, send_sem, recv_sem, device_id):
+    copy = pltpu.make_async_remote_copy(
+        src_ref=src,
+        dst_ref=dst,
+        send_sem=send_sem,
+        recv_sem=recv_sem,
+        device_id=device_id,
+        device_id_type=pl.DeviceIdType.MESH,
+    )
+    copy.start()
+    return copy
+
+
+def meet(n, me, half):
+    barrier = pltpu.get_barrier_semaphore()
+    for offset in range(1, n):
+        pl.semaphore_signal(
+            barrier,
+            inc=1,
+            device_id={"tensor": flip(me, offset)},
+            device_id_type=pl.DeviceIdType.MESH,
+        )
+    count = n - 1
+    if half is not None:
+        pl.semaphore_signal(
+            barrier, inc=1, device_id={"dp": 1 - half}, device_id_type=pl.DeviceIdType.MESH
+        )
+        count += 1
+    pl.semaphore_wait(barrier, count)
+
+
+def scatter_sums(n, me, part, slots, send, recv):
+    rows = part.shape[1] // n
+    copies = []
+    for offset in range(1, n):
+        peer = flip(me, offset)
+        at = pl.ds(pl.multiple_of(peer * rows, rows), rows)
+        copies.append(
+            remote(
+                part.at[:, at, :],
+                slots.at[offset],
+                send.at[0, offset],
+                recv.at[0, offset],
+                {"tensor": peer},
+            )
+        )
+    return copies
+
+
+def gather_sums(n, me, part, slots, total, send, recv, copies):
+    rows = part.shape[1] // n
+    mine = pl.ds(pl.multiple_of(me * rows, rows), rows)
+    for copy in copies:
+        copy.wait()
+    summed = part[:, mine, :]
+    for offset in range(1, n):
+        summed = summed + slots[offset]
+    total[:, mine, :] = summed.astype(BF16)
+    return [
+        remote(
+            total.at[:, mine, :],
+            total.at[:, mine, :],
+            send.at[1, offset],
+            recv.at[1, offset],
+            {"tensor": flip(me, offset)},
+        )
+        for offset in range(1, n)
+    ]
+
+
+def fetch_kernel(
+    n, levels, x_ref, c_ref, uu_ref, ud_ref, xg, cg, low, part, slots, send, recv, psend, precv
+):
+    me = lax.axis_index("tensor")
+    meet(n, me, None)
+    part[0] = tn(x_ref[...], uu_ref[...])
+    part[1] = tn(c_ref[...], ud_ref[...])
+    sums = scatter_sums(n, me, part, slots, send, recv)
+    panels = []
+    for level in reversed(range(levels)):
+        for kind, (src, dst) in enumerate(((x_ref, xg), (c_ref, cg))):
+            panels.append(
+                remote(
+                    src,
+                    dst.at[level + 1],
+                    psend.at[kind, level],
+                    precv.at[kind, level],
+                    {"tensor": flip(me, 1 << level)},
+                )
+            )
+    xg[0] = x_ref[...]
+    cg[0] = c_ref[...]
+    rows = gather_sums(n, me, part, slots, low, send, recv, sums)
+    for copy in panels + rows:
+        copy.wait()
+
+
+def fetch(n, levels, features, cotangent, u_up, u_down):
+    dim, tokens = features.shape
+    rank = u_up.shape[1]
+    vmem = pl.BlockSpec(memory_space=pltpu.VMEM)
+    return pl.pallas_call(
+        functools.partial(fetch_kernel, n, levels),
+        out_shape=(
+            jax.ShapeDtypeStruct((levels + 1, dim, tokens), BF16),
+            jax.ShapeDtypeStruct((levels + 1, dim, tokens), BF16),
+            jax.ShapeDtypeStruct((2, tokens, rank), BF16),
+        ),
+        in_specs=[vmem] * 4,
+        out_specs=(vmem,) * 3,
+        scratch_shapes=[
+            pltpu.VMEM((2, tokens, rank), F32),
+            pltpu.VMEM((n, 2, tokens // n, rank), F32),
+            pltpu.SemaphoreType.DMA((2, n)),
+            pltpu.SemaphoreType.DMA((2, n)),
+            pltpu.SemaphoreType.DMA((2, levels)),
+            pltpu.SemaphoreType.DMA((2, levels)),
+        ],
+        compiler_params=pltpu.CompilerParams(
+            collective_id=0, has_side_effects=True, vmem_limit_bytes=VMEM_BYTES
+        ),
+    )(features, cotangent, u_up, u_down)
+
+
+def hidden_kernel(
+    slot_count,
+    block,
+    steps,
+    tables,
+    xg,
+    cg,
+    low,
+    wu,
+    wd,
+    vu,
+    vd,
+    act_out,
+    pre_out,
+    part,
+    own,
+    away,
+    xt,
+    ct,
+    back,
+):
+    step = pl.program_id(0)
+    per_panel = xg.shape[1] // block
+    tokens = xg.shape[2]
+
+    @pl.when(step == 0)
+    def _():
+        for slot in range(slot_count):
+            for b in range(per_panel):
+                rows = slice(b * block, (b + 1) * block)
+                xt[slot, b] = xg[slot, rows, :].T
+                ct[slot, b] = cg[slot, rows, :].T
+        part[...] = jnp.zeros_like(part)
+        back[...] = jnp.zeros_like(back)
+
+    up = [tables[0, slot, step] for slot in range(slot_count)]
+    down = [tables[1, slot, step] for slot in range(slot_count)]
+    pre = nt(low[0], vu[...])
+    grad = nt(low[1], vd[...])
+    for slot in range(slot_count):
+        pre = pre + nn(xt[slot, up[slot]], wu[slot])
+        grad = grad + nn(ct[slot, down[slot]], wd[slot])
+    cdf = 0.5 * (1.0 + lax.erf(pre * root_half))
+    act = (pre * cdf).astype(BF16)
+    grad_pre = (grad * (cdf + pre * jnp.exp(-0.5 * pre * pre) * inv_root_tau)).astype(BF16)
+    act_out[...] = act
+    pre_out[...] = grad_pre
+    part[0] += nn(act, vd[...])
+    part[1] += nn(grad_pre, vu[...])
+    for slot in range(slot_count):
+        back[slot, 0, down[slot]] += nt(wd[slot], act)
+        back[slot, 1, up[slot]] += nt(wu[slot], grad_pre)
+
+    @pl.when(step == steps - 1)
+    def _():
+        for kind in range(2):
+            for b in range(per_panel):
+                rows = slice(b * block, (b + 1) * block)
+                own[kind, rows, :] = back[0, kind, b]
+                for slot in range(1, slot_count):
+                    away[slot - 1, kind, rows, :] = back[slot, kind, b].astype(BF16)
+
+
+def hidden_pass(tables, xg, cg, low, w_up, w_down, v_up, v_down):
+    slot_count, block, hidden = w_up.shape
+    _, dim, tokens = xg.shape
+    rank = v_up.shape[1]
+    steps = hidden // block
+    per_panel = dim // block
+    whole = lambda *shape: pl.BlockSpec(shape, lambda c, *_: (0,) * len(shape))
+    return pl.pallas_call(
+        functools.partial(hidden_kernel, slot_count, block, steps),
+        out_shape=(
+            jax.ShapeDtypeStruct((tokens, hidden), BF16),
+            jax.ShapeDtypeStruct((tokens, hidden), BF16),
+            jax.ShapeDtypeStruct((2, tokens, rank), F32),
+            jax.ShapeDtypeStruct((2, dim, tokens), F32),
+            jax.ShapeDtypeStruct((slot_count - 1, 2, dim, tokens), BF16),
+        ),
+        grid_spec=pltpu.PrefetchScalarGridSpec(
+            num_scalar_prefetch=1,
+            grid=(steps,),
+            in_specs=[
+                whole(slot_count, dim, tokens),
+                whole(slot_count, dim, tokens),
+                whole(2, tokens, rank),
+                pl.BlockSpec((slot_count, block, block), lambda c, *_: (0, 0, c)),
+                pl.BlockSpec((slot_count, block, block), lambda c, *_: (0, 0, c)),
+                pl.BlockSpec((block, rank), lambda c, *_: (c, 0)),
+                pl.BlockSpec((block, rank), lambda c, *_: (c, 0)),
+            ],
+            out_specs=(
+                pl.BlockSpec((tokens, block), lambda c, *_: (0, c)),
+                pl.BlockSpec((tokens, block), lambda c, *_: (0, c)),
+                whole(2, tokens, rank),
+                whole(2, dim, tokens),
+                whole(slot_count - 1, 2, dim, tokens),
+            ),
+            scratch_shapes=[
+                pltpu.VMEM((slot_count, per_panel, tokens, block), BF16),
+                pltpu.VMEM((slot_count, per_panel, tokens, block), BF16),
+                pltpu.VMEM((slot_count, 2, per_panel, block, tokens), F32),
+            ],
+        ),
+        compiler_params=pltpu.CompilerParams(vmem_limit_bytes=VMEM_BYTES),
+    )(tables, xg, cg, low, w_up, w_down, v_up, v_down)
+
+
+def return_kernel(
+    n,
+    levels,
+    block,
+    away,
+    part_ref,
+    act,
+    pre,
+    xg,
+    cg,
+    low_first,
+    home,
+    low,
+    act_p,
+    pre_p,
+    x_p,
+    c_p,
+    xown_p,
+    cown_p,
+    lowf_p,
+    low_p,
+    slots,
+    send,
+    recv,
+    psend,
+    precv,
+    dsend,
+    drecv,
+):
+    me = lax.axis_index("tensor")
+    half = lax.axis_index("dp")
+    twin = {"dp": 1 - half}
+    meet(n, me, half)
+    sums = scatter_sums(n, me, part_ref, slots, send, recv)
+    panels = []
+    for level in reversed(range(levels)):
+        panels.append(
+            remote(
+                away.at[level],
+                home.at[level],
+                psend.at[level],
+                precv.at[level],
+                {"tensor": flip(me, 1 << level)},
+            )
+        )
+    rows = block // 2
+    twins = []
+    pairs = [(act, act_p), (pre, pre_p), (low_first, lowf_p), (xg.at[0], xown_p), (cg.at[0], cown_p)]
+    for b in range(xg.shape[1] // block):
+        at = pl.ds(pl.multiple_of(b * block + (1 - half) * rows, rows), rows)
+        pairs.append((xg.at[:, at, :], x_p.at[:, b]))
+        pairs.append((cg.at[:, at, :], c_p.at[:, b]))
+    for k, (src, dst) in enumerate(pairs):
+        twins.append(remote(src, dst, dsend.at[k], drecv.at[k], twin))
+    gathered = gather_sums(n, me, part_ref, slots, low, send, recv, sums)
+    for copy in gathered:
+        copy.wait()
+    last = len(pairs)
+    twins.append(remote(low, low_p, dsend.at[last], drecv.at[last], twin))
+    for copy in panels + twins:
+        copy.wait()
+
+
+def send_back(n, levels, block, away, part, act, pre, xg, cg, low_first):
+    _, dim, tokens = xg.shape
+    rank = part.shape[2]
+    per_panel = dim // block
+    vmem = pl.BlockSpec(memory_space=pltpu.VMEM)
+    shape = lambda *s: jax.ShapeDtypeStruct(s, BF16)
+    copies = 6 + 2 * per_panel
+    return pl.pallas_call(
+        functools.partial(return_kernel, n, levels, block),
+        out_shape=(
+            shape(*away.shape),
+            shape(2, tokens, rank),
+            shape(*act.shape),
+            shape(*pre.shape),
+            shape(levels + 1, per_panel, block // 2, tokens),
+            shape(levels + 1, per_panel, block // 2, tokens),
+            shape(dim, tokens),
+            shape(dim, tokens),
+            shape(2, tokens, rank),
+            shape(2, tokens, rank),
+        ),
+        in_specs=[vmem] * 7,
+        out_specs=(vmem,) * 10,
+        scratch_shapes=[
+            pltpu.VMEM((n, 2, tokens // n, rank), F32),
+            pltpu.SemaphoreType.DMA((2, n)),
+            pltpu.SemaphoreType.DMA((2, n)),
+            pltpu.SemaphoreType.DMA((levels,)),
+            pltpu.SemaphoreType.DMA((levels,)),
+            pltpu.SemaphoreType.DMA((copies,)),
+            pltpu.SemaphoreType.DMA((copies,)),
+        ],
+        compiler_params=pltpu.CompilerParams(
+            collective_id=1, has_side_effects=True, vmem_limit_bytes=VMEM_BYTES
+        ),
+    )(away, part, act, pre, xg, cg, low_first)
+
+
+def final_kernel(
+    slot_count,
+    block,
+    tables,
+    xg,
+    cg,
+    x_p,
+    c_p,
+    xown_p,
+    cown_p,
+    lowf,
+    low,
+    lowf_p,
+    low_p,
+    own,
+    home,
+    uu,
+    ud,
+    act,
+    pre,
+    act_p,
+    pre_p,
+    out,
+    gfeat,
+    gwu,
+    gwd,
+    guu,
+    gvu,
+    gud,
+    gvd,
+):
+    step = pl.program_id(0)
+    half = tables[2, 0, 0]
+    rows = block // 2
+    width = lowf.shape[2] // 2
+    cols = pl.ds(pl.multiple_of(half * width, width), width)
+    for slot in range(slot_count):
+        for table, mine, twin, hid, hid_p, grad in (
+            (0, xg, x_p, pre, pre_p, gwu),
+            (1, cg, c_p, act, act_p, gwd),
+        ):
+            b = tables[table, slot, step]
+            at = pl.ds(pl.multiple_of(b * block + half * rows, rows), rows)
+            grad[slot] = nn(mine[slot, at, :], hid[...]) + nn(twin[slot, b], hid_p[...])
+    gvu[...] = tn(pre[...], lowf[0, :, cols]) + tn(pre_p[...], lowf_p[0, :, cols])
+    gvd[...] = tn(act[...], lowf[1, :, cols]) + tn(act_p[...], lowf_p[1, :, cols])
+
+    @pl.when(step == 0)
+    def _():
+        for kind, u, result in ((0, ud, out), (1, uu, gfeat)):
+            total = own[kind] + nt(u[...], low[kind])
+            for level in range(slot_count - 1):
+                total = total + home[level, kind].astype(F32)
+            result[...] = total.astype(BF16)
+        guu[...] = nn(xg[0], low[1, :, cols]) + nn(xown_p[...], low_p[1, :, cols])
+        gud[...] = nn(cg[0], low[0, :, cols]) + nn(cown_p[...], low_p[0, :, cols])
+
+
+def finish(tables, xg, cg, x_p, c_p, xown_p, cown_p, lowf, low, lowf_p, low_p, own, home, u_up, u_down,
+           act, pre, act_p, pre_p, block):
+    slot_count, dim, tokens = xg.shape
+    hidden = act.shape[1]
+    rank = lowf.shape[2]
+    full = lambda a: pl.BlockSpec(a.shape, lambda c, *_: (0,) * a.ndim)
+    hid = pl.BlockSpec((tokens, block), lambda c, *_: (0, c))
+    gw = pl.BlockSpec((slot_count, block // 2, block), lambda c, *_: (0, 0, c))
+    gv = pl.BlockSpec((block, rank // 2), lambda c, *_: (c, 0))
+    once = lambda *shape: pl.BlockSpec(shape, lambda c, *_: (0,) * len(shape))
+    fixed = (xg, cg, x_p, c_p, xown_p, cown_p, lowf, low, lowf_p, low_p, own, home, u_up, u_down)
+    return pl.pallas_call(
+        functools.partial(final_kernel, slot_count, block),
+        out_shape=(
+            jax.ShapeDtypeStruct((dim, tokens), BF16),
+            jax.ShapeDtypeStruct((dim, tokens), BF16),
+            jax.ShapeDtypeStruct((slot_count, block // 2, hidden), F32),
+            jax.ShapeDtypeStruct((slot_count, block // 2, hidden), F32),
+            jax.ShapeDtypeStruct((dim, rank // 2), F32),
+            jax.ShapeDtypeStruct((hidden, rank // 2), F32),
+            jax.ShapeDtypeStruct((dim, rank // 2), F32),
+            jax.ShapeDtypeStruct((hidden, rank // 2), F32),
+        ),
+        grid_spec=pltpu.PrefetchScalarGridSpec(
+            num_scalar_prefetch=1,
+            grid=(hidden // block,),
+            in_specs=[full(a) for a in fixed] + [hid] * 4,
+            out_specs=(
+                once(dim, tokens),
+                once(dim, tokens),
+                gw,
+                gw,
+                once(dim, rank // 2),
+                gv,
+                once(dim, rank // 2),
+                gv,
+            ),
+        ),
+        compiler_params=pltpu.CompilerParams(vmem_limit_bytes=VMEM_BYTES),
+    )(tables, *fixed, act, pre, act_p, pre_p)
+
+
+def one_panel_each(
+    features, table_up, table_down, w_up, u_up, v_up, w_down, u_down, v_down, cotangent
+):
+    slot_count, block, hidden = w_up.shape
+    levels = slot_count - 1
+    n = lax.axis_size("tensor")
+    me = lax.axis_index("tensor")
+    count = hidden // block
+    tables = lax.dynamic_slice_in_dim(jnp.stack([table_up, table_down]), me * count, count, 2)
+    half = jnp.full((1,) + tables.shape[1:], lax.axis_index("dp"), jnp.int32)
+    tables = jnp.concatenate([tables, half])
+    xg, cg, lowf = fetch(n, levels, features, cotangent, u_up, u_down)
+    act, pre, part, own, away = hidden_pass(tables, xg, cg, lowf, w_up, w_down, v_up, v_down)
+    home, low, act_p, pre_p, x_p, c_p, xown_p, cown_p, lowf_p, low_p = send_back(
+        n, levels, block, away, part, act, pre, xg, cg, lowf
+    )
+    return finish(tables, xg, cg, x_p, c_p, xown_p, cown_p, lowf, low, lowf_p, low_p, own, home,
+                  u_up, u_down, act, pre, act_p, pre_p, block)
+
+
+def solve(*args):
+    slot_count = args[3].shape[0]
+    fits = (
+        lax.axis_size("tensor") == 1 << slot_count - 1
+        and lax.axis_size("dp") == 2
+        and args[3].shape[2] % args[3].shape[1] == 0
+    )
+    return one_panel_each(*args) if fits else on_device(*args)
+
+
 def solution(mesh):
     return jax.shard_map(
-        on_device,
+        solve,
         mesh=mesh,
         in_specs=(
             P("tensor", ("groups", "dp")),

time: 476 us -> 132 us (0.28); the launches traced: 467 us -> 131 us
  waiting for transfers between devices: 146 us -> 0 us
  Pallas kernels: 0 us -> 129 us
  blocking collectives: 126 us -> 0 us
  local copies, waits for them, and re-layouts: 101 us -> 0.6 us
  matrix products: 47.6 us -> 0 us
  other arithmetic: 16.4 us -> 0.78 us
  between operations: 15.1 us -> 0.66 us
  starting transfers between devices: 14.3 us -> 0 us
    ppermute x12 -> x0, waiting for transfers between devices: 146 us -> none  [from_partner(): lax.ppermute(array, axis, [(i, i ^ 1 << distance) for i in range(lax.axis...]
    pallas_call x0 -> x4, Pallas kernels: none -> 129 us  [the longest x1 50.3 us: send_back(): pl.pallas_call(functools.partial(return_kernel, n, levels, block), out_sh...]
    psum x2 -> x0, blocking collectives: 126 us -> none  [the longest x1 86.1 us: on_device(): lax.psum(jnp.dot(u_up.T, features, preferred_element_type=jnp.float32), '...]
    dot_general x26 -> x0, matrix products: 47.6 us -> none  [the longest x8 11.8 us: place_blocks(): jnp.einsum('bn,brt->nrt', onehot, portion, precision=lax.Precision.HIGHEST)]
    unnamed x89 -> x0, local copies, waits for them, and re-layouts: 29.3 us -> none
    ppermute x6 -> x0, local copies, waits for them, and re-layouts: 16.7 us -> none  [from_partner(): lax.ppermute(array, axis, [(i, i ^ 1 << distance) for i in range(lax.axis...]
    reshape x5 -> x0, local copies, waits for them, and re-layouts: 16.5 us -> none  [the longest x1 7.45 us: on_device(): w_down.reshape(slot_count, block_rows, block_count, column_width)]
    gather x16 -> x0, local copies, waits for them, and re-layouts: 15.9 us -> none  [the longest x8 10.7 us: pick_blocks(): return jnp.take(stacked, chosen, axis=0)]
  transfers between devices with their start and end apart: 18 -> 0, of which waited for: 4 -> 0; matrix products, arithmetic and copies ran while one was open for 30% -> 0% of each run, Pallas kernels for 0% -> 0%
where the time goes in v1:
time: 132 us; the launch traced here: 131 us
  Pallas kernels  129 us (98%)
    pallas_call x1, Pallas kernels, send_back(): pl.pallas_call(functools.partial(return_kernel, n, levels, block), out_sh...  50.3 us
    pallas_call x1, Pallas kernels, fetch(): pl.pallas_call(functools.partial(fetch_kernel, n, levels), out_shape=(jax...  49 us
    pallas_call x1, Pallas kernels, hidden_pass(): pl.pallas_call(functools.partial(hidden_kernel, slot_count, block, steps)...  15.3 us
    pallas_call x1, Pallas kernels, finish(): pl.pallas_call(functools.partial(final_kernel, slot_count, block), out_sh...  14.7 us

profile of v1, /device:TPU:0, one launch (start us, length us, event | category | flops | bytes accessed | tf_op | source)
XLA Modules:
  0.0 131.2 jit_solution(7961356504293872789)
XLA Ops:
  0.6 0.8 dynamic-slice_add_fusion
  1.4 0.6 concatenate.3.tables
  2.0 49.0 %shard_map.161 = (bf16[4,512,256]{2,1,0:T(8,128)(2,1)}, bf16[4,512,256]{2,1,0:T(8,128)(2,1)}, bf16[2,256,256]{2,1,0:T(8,128)(2,1)}) custom-call(bf16[512,256]{1,0:T(8,128)(2,1)} %x_ref.1, bf16[512,256]{1,0:T(8,128)(2,1)} %c_ref.1, bf16[512,256]{1,0:T(8,128)(2,1)} %uu.1, bf16[512,256]{1,0:T(8,128)(2,1)} %ud.1), custom_call_target="tpu_custom_call" | custom-call | tf_op jit(solution)/shard_map/pallas_call | solution.py:332
  51.0 15.3 %shard_map.162 = (bf16[256,2048]{1,0:T(8,128)(2,1)}, bf16[256,2048]{1,0:T(8,128)(2,1)}, f32[2,256,256]{2,1,0:T(8,128)}, f32[2,512,256]{2,1,0:T(8,128)}, bf16[3,2,512,256]{3,2,1,0:T(8,128)(2,1)}) custom-call(s32[3,4,8]{2,1,0:T(4,128)} %concatenate.3.tables, bf16[4,512,256]{2,1,0:T(8,128)(2,1)} %get-tuple-element.26.xg, ...), custom_call_target="tpu_custom_call" | custom-call | tf_op jit(solution)/shard_map/pallas_call | solution.py:425
  66.3 50.3 %shard_map.163 = (bf16[3,2,512,256]{3,2,1,0:T(8,128)(2,1)}, bf16[2,256,256]{2,1,0:T(8,128)(2,1)}, bf16[256,2048]{1,0:T(8,128)(2,1)}, bf16[256,2048]{1,0:T(8,128)...) custom-call(bf16[3,2,512,256]{3,2,1,0:T(8,128)(2,1)} %get-tuple-elem, ...), custom_call_target="tpu_custom_call" | custom-call | tf_op jit(solution)/shard_map/pallas_call | solution.py:533
  116.6 14.7 %shard_map.164 = (bf16[512,256]{1,0:T(8,128)(2,1)}, bf16[512,256]{1,0:T(8,128)(2,1)}, f32[4,128,2048]{2,1,0:T(8,128)}, f32[4,128,2048]{2,1,0:T(8,128)}, f32[512,...) custom-call(s32[3,4,8]{2,1,0:T(4,128)} %concatenate.3.tables, ...), custom_call_target="tpu_custom_call" | custom-call | tf_op jit(solution)/shard_map/pallas_call | solution.py:633

commit v2 on v1

--- a/solution.py
+++ b/solution.py
@@ -259,15 +259,17 @@
     pl.semaphore_wait(barrier, count)
 
 
-def scatter_sums(n, me, part, slots, send, recv):
-    rows = part.shape[1] // n
+def scatter_sums(n, me, part, rounded, slots, send, recv):
+    group = n // 2
+    rows = part.shape[1] // group
+    rounded[...] = part[...].astype(BF16)
     copies = []
-    for offset in range(1, n):
+    for offset in range(1, group):
         peer = flip(me, offset)
-        at = pl.ds(pl.multiple_of(peer * rows, rows), rows)
+        at = pl.ds(pl.multiple_of(peer % group * rows, rows), rows)
         copies.append(
             remote(
-                part.at[:, at, :],
+                rounded.at[:, at, :],
                 slots.at[offset],
                 send.at[0, offset],
                 recv.at[0, offset],
@@ -277,15 +279,27 @@
     return copies
 
 
-def gather_sums(n, me, part, slots, total, send, recv, copies):
-    rows = part.shape[1] // n
-    mine = pl.ds(pl.multiple_of(me * rows, rows), rows)
+def cross_sums(n, me, part, slots, pair, send, recv, copies):
+    group = n // 2
+    rows = part.shape[1] // group
+    mine = pl.ds(pl.multiple_of(me % group * rows, rows), rows)
     for copy in copies:
         copy.wait()
     summed = part[:, mine, :]
-    for offset in range(1, n):
-        summed = summed + slots[offset]
-    total[:, mine, :] = summed.astype(BF16)
+    for offset in range(1, group):
+        summed = summed + slots[offset].astype(F32)
+    pair[0] = summed.astype(BF16)
+    return remote(
+        pair.at[0], pair.at[1], send.at[0, 0], recv.at[0, 0], {"tensor": flip(me, group)}
+    )
+
+
+def gather_sums(n, me, pair, total, send, recv, copy):
+    group = n // 2
+    rows = pair.shape[2]
+    mine = pl.ds(pl.multiple_of(me % group * rows, rows), rows)
+    copy.wait()
+    total[:, mine, :] = (pair[0].astype(F32) + pair[1].astype(F32)).astype(BF16)
     return [
         remote(
             total.at[:, mine, :],
@@ -294,18 +308,29 @@
             recv.at[1, offset],
             {"tensor": flip(me, offset)},
         )
-        for offset in range(1, n)
+        for offset in range(1, group)
     ]
 
 
+def sum_scratch(n, tokens, rank):
+    group = n // 2
+    return [
+        pltpu.VMEM((2, tokens, rank), BF16),
+        pltpu.VMEM((group, 2, tokens // group, rank), BF16),
+        pltpu.VMEM((2, 2, tokens // group, rank), BF16),
+        pltpu.SemaphoreType.DMA((2, group)),
+        pltpu.SemaphoreType.DMA((2, group)),
+    ]
+
+
 def fetch_kernel(
-    n, levels, x_ref, c_ref, uu_ref, ud_ref, xg, cg, low, part, slots, send, recv, psend, precv
+    n, levels, x_ref, c_ref, uu_ref, ud_ref, xg, cg, low, part, rounded, slots, pair, send, recv, psend, precv
 ):
     me = lax.axis_index("tensor")
     meet(n, me, None)
     part[0] = tn(x_ref[...], uu_ref[...])
     part[1] = tn(c_ref[...], ud_ref[...])
-    sums = scatter_sums(n, me, part, slots, send, recv)
+    sums = scatter_sums(n, me, part, rounded, slots, send, recv)
     panels = []
     for level in reversed(range(levels)):
         for kind, (src, dst) in enumerate(((x_ref, xg), (c_ref, cg))):
@@ -320,7 +345,8 @@
             )
     xg[0] = x_ref[...]
     cg[0] = c_ref[...]
-    rows = gather_sums(n, me, part, slots, low, send, recv, sums)
+    crossing = cross_sums(n, me, part, slots, pair, send, recv, sums)
+    rows = gather_sums(n, me, pair, low, send, recv, crossing)
     for copy in panels + rows:
         copy.wait()
 
@@ -340,9 +366,7 @@
         out_specs=(vmem,) * 3,
         scratch_shapes=[
             pltpu.VMEM((2, tokens, rank), F32),
-            pltpu.VMEM((n, 2, tokens // n, rank), F32),
-            pltpu.SemaphoreType.DMA((2, n)),
-            pltpu.SemaphoreType.DMA((2, n)),
+            *sum_scratch(n, tokens, rank),
             pltpu.SemaphoreType.DMA((2, levels)),
             pltpu.SemaphoreType.DMA((2, levels)),
         ],
@@ -481,7 +505,9 @@
     cown_p,
     lowf_p,
     low_p,
+    rounded,
     slots,
+    pair,
     send,
     recv,
     psend,
@@ -493,7 +519,7 @@
     half = lax.axis_index("dp")
     twin = {"dp": 1 - half}
     meet(n, me, half)
-    sums = scatter_sums(n, me, part_ref, slots, send, recv)
+    sums = scatter_sums(n, me, part_ref, rounded, slots, send, recv)
     panels = []
     for level in reversed(range(levels)):
         panels.append(
@@ -514,7 +540,8 @@
         pairs.append((cg.at[:, at, :], c_p.at[:, b]))
     for k, (src, dst) in enumerate(pairs):
         twins.append(remote(src, dst, dsend.at[k], drecv.at[k], twin))
-    gathered = gather_sums(n, me, part_ref, slots, low, send, recv, sums)
+    crossing = cross_sums(n, me, part_ref, slots, pair, send, recv, sums)
+    gathered = gather_sums(n, me, pair, low, send, recv, crossing)
     for copy in gathered:
         copy.wait()
     last = len(pairs)
@@ -547,9 +574,7 @@
         in_specs=[vmem] * 7,
         out_specs=(vmem,) * 10,
         scratch_shapes=[
-            pltpu.VMEM((n, 2, tokens // n, rank), F32),
-            pltpu.SemaphoreType.DMA((2, n)),
-            pltpu.SemaphoreType.DMA((2, n)),
+            *sum_scratch(n, tokens, rank),
             pltpu.SemaphoreType.DMA((levels,)),
             pltpu.SemaphoreType.DMA((levels,)),
             pltpu.SemaphoreType.DMA((copies,)),
@@ -684,7 +709,8 @@
 def solve(*args):
     slot_count = args[3].shape[0]
     fits = (
-        lax.axis_size("tensor") == 1 << slot_count - 1
+        slot_count > 1
+        and lax.axis_size("tensor") == 1 << slot_count - 1
         and lax.axis_size("dp") == 2
         and args[3].shape[2] % args[3].shape[1] == 0
     )

time: 132 us -> 116 us (0.88)
  Pallas kernels: 129 us -> 114 us
    pallas_call x1, Pallas kernels: 49 us -> 40.8 us  [fetch(): pl.pallas_call(functools.partial(fetch_kernel, n, levels), out_shape=(jax...]
    pallas_call x1, Pallas kernels: 50.3 us -> 43.1 us  [send_back(): pl.pallas_call(functools.partial(return_kernel, n, levels, block), out_sh...]
where the time goes in v2:
time: 116 us
  Pallas kernels  114 us (98%)
    pallas_call x1, Pallas kernels, send_back(): pl.pallas_call(functools.partial(return_kernel, n, levels, block), out_sh...  43.1 us
    pallas_call x1, Pallas kernels, fetch(): pl.pallas_call(functools.partial(fetch_kernel, n, levels), out_shape=(jax...  40.8 us
    pallas_call x1, Pallas kernels, hidden_pass(): pl.pallas_call(functools.partial(hidden_kernel, slot_count, block, steps)...  15.3 us
    pallas_call x1, Pallas kernels, finish(): pl.pallas_call(functools.partial(final_kernel, slot_count, block), out_sh...  14.7 us

profile of v2, /device:TPU:0, one launch (start us, length us, event | category | flops | bytes accessed | tf_op | source)
XLA Modules:
  0.0 115.8 jit_solution(16860125308259679899)
XLA Ops:
  0.6 0.8 dynamic-slice_add_fusion
  1.4 0.6 concatenate.3.tables
  2.0 40.8 %shard_map.161 = (bf16[4,512,256]{2,1,0:T(8,128)(2,1)}, bf16[4,512,256]{2,1,0:T(8,128)(2,1)}, bf16[2,256,256]{2,1,0:T(8,128)(2,1)}) custom-call(bf16[512,256]{1,0:T(8,128)(2,1)} %x_ref.1, bf16[512,256]{1,0:T(8,128)(2,1)} %c_ref.1, bf16[512,256]{1,0:T(8,128)(2,1)} %uu.1, bf16[512,256]{1,0:T(8,128)(2,1)} %ud.1), custom_call_target="tpu_custom_call" | custom-call | tf_op jit(solution)/shard_map/pallas_call | solution.py:358
  42.8 15.3 %shard_map.162 = (bf16[256,2048]{1,0:T(8,128)(2,1)}, bf16[256,2048]{1,0:T(8,128)(2,1)}, f32[2,256,256]{2,1,0:T(8,128)}, f32[2,512,256]{2,1,0:T(8,128)}, bf16[3,2,512,256]{3,2,1,0:T(8,128)(2,1)}) custom-call(s32[3,4,8]{2,1,0:T(4,128)} %concatenate.3.tables, bf16[4,512,256]{2,1,0:T(8,128)(2,1)} %get-tuple-element.26.xg, ...), custom_call_target="tpu_custom_call" | custom-call | tf_op jit(solution)/shard_map/pallas_call | solution.py:449
  58.1 43.1 %shard_map.163 = (bf16[3,2,512,256]{3,2,1,0:T(8,128)(2,1)}, bf16[2,256,256]{2,1,0:T(8,128)(2,1)}, bf16[256,2048]{1,0:T(8,128)(2,1)}, bf16[256,2048]{1,0:T(8,128)...) custom-call(bf16[3,2,512,256]{3,2,1,0:T(8,128)(2,1)} %get-tuple-elem, ...), custom_call_target="tpu_custom_call" | custom-call | tf_op jit(solution)/shard_map/pallas_call | solution.py:560
  101.1 14.7 %shard_map.164 = (bf16[512,256]{1,0:T(8,128)(2,1)}, bf16[512,256]{1,0:T(8,128)(2,1)}, f32[4,128,2048]{2,1,0:T(8,128)}, f32[4,128,2048]{2,1,0:T(8,128)}, f32[512,...) custom-call(s32[3,4,8]{2,1,0:T(4,128)} %concatenate.3.tables, ...), custom_call_target="tpu_custom_call" | custom-call | tf_op jit(solution)/shard_map/pallas_call | solution.py:658

commit v3 on v0

--- a/solution.py
+++ b/solution.py
@@ -1,8 +1,11 @@
+import functools
 import math
 
 import jax
 import jax.numpy as jnp
 from jax import lax
+from jax.experimental import pallas as pl
+from jax.experimental.pallas import tpu as pltpu
 from jax.sharding import PartitionSpec as P
 
 root_half = 1.0 / math.sqrt(2.0)
@@ -201,9 +204,460 @@
     )
 
 
+F32, BF16 = jnp.float32, jnp.bfloat16
+VMEM_BYTES = 56 * 2**20
+
+
+def nn(a, b):
+    return lax.dot_general(a, b, (((1,), (0,)), ((), ())), preferred_element_type=F32)
+
+
+def nt(a, b):
+    return lax.dot_general(a, b, (((1,), (1,)), ((), ())), preferred_element_type=F32)
+
+
+def tn(a, b):
+    return lax.dot_general(a, b, (((0,), (0,)), ((), ())), preferred_element_type=F32)
+
+
+def flip(me, offset):
+    peer = me
+    for k in range(offset.bit_length()):
+        if offset >> k & 1:
+            peer = peer + (1 << k) * (1 - 2 * ((me // (1 << k)) % 2))
+    return peer
+
+
+def remote(src, dst, send_sem, recv_sem, device_id):
+    copy = pltpu.make_async_remote_copy(
+        src_ref=src,
+        dst_ref=dst,
+        send_sem=send_sem,
+        recv_sem=recv_sem,
+        device_id=device_id,
+        device_id_type=pl.DeviceIdType.MESH,
+    )
+    copy.start()
+    return copy
+
+
+def meet(n, me, half):
+    barrier = pltpu.get_barrier_semaphore()
+    for offset in range(1, n):
+        pl.semaphore_signal(
+            barrier,
+            inc=1,
+            device_id={"tensor": flip(me, offset)},
+            device_id_type=pl.DeviceIdType.MESH,
+        )
+    count = n - 1
+    if half is not None:
+        pl.semaphore_signal(
+            barrier, inc=1, device_id={"dp": 1 - half}, device_id_type=pl.DeviceIdType.MESH
+        )
+        count += 1
+    pl.semaphore_wait(barrier, count)
+
+
+def scatter_sums(n, me, part, slots, send, recv):
+    group = n // 2
+    rows = part.shape[1] // group
+    copies = []
+    for offset in range(1, group):
+        peer = flip(me, offset)
+        at = pl.ds(pl.multiple_of(peer % group * rows, rows), rows)
+        copies.append(
+            remote(
+                part.at[:, at, :],
+                slots.at[offset],
+                send.at[0, offset],
+                recv.at[0, offset],
+                {"tensor": peer},
+            )
+        )
+    return copies
+
+
+def cross_sums(n, me, part, slots, pair, send, recv, copies):
+    group = n // 2
+    rows = part.shape[1] // group
+    mine = pl.ds(pl.multiple_of(me % group * rows, rows), rows)
+    for copy in copies:
+        copy.wait()
+    summed = part[:, mine, :]
+    for offset in range(1, group):
+        summed = summed + slots[offset]
+    pair[0] = summed
+    return remote(
+        pair.at[0], pair.at[1], send.at[0, 0], recv.at[0, 0], {"tensor": flip(me, group)}
+    )
+
+
+def gather_sums(n, me, pair, total, send, recv, copy):
+    group = n // 2
+    rows = pair.shape[2]
+    mine = pl.ds(pl.multiple_of(me % group * rows, rows), rows)
+    copy.wait()
+    total[:, mine, :] = (pair[0] + pair[1]).astype(BF16)
+    return [
+        remote(
+            total.at[:, mine, :],
+            total.at[:, mine, :],
+            send.at[1, offset],
+            recv.at[1, offset],
+            {"tensor": flip(me, offset)},
+        )
+        for offset in range(1, group)
+    ]
+
+
+def sum_scratch(n, lead, tokens, rank):
+    group = n // 2
+    return [
+        pltpu.VMEM((lead, tokens, rank), F32),
+        pltpu.VMEM((group, lead, tokens // group, rank), F32),
+        pltpu.VMEM((2, lead, tokens // group, rank), F32),
+        pltpu.SemaphoreType.DMA((2, group)),
+        pltpu.SemaphoreType.DMA((2, group)),
+    ]
+
+
+def layer_kernel(n, levels, block, tables, x_ref, c_ref, uu, ud, wu_any, wd_any, vu_any, vd_any, *refs):
+    (xg, cg, lowf, act, pre, own, home, low_a, low_b, act_p, pre_p, x_p, c_p) = refs[:13]
+    (xown_p, cown_p, lowf_p, lowa_p, lowb_p) = refs[13:18]
+    first, second, third = refs[18:23], refs[23:28], refs[28:33]
+    (wu, wd, vu, vd, xt, ct, slope, acc, away, lsem, psend, precv, dsend, drecv) = refs[33:]
+    me = lax.axis_index("tensor")
+    half = lax.axis_index("dp")
+    twin = {"dp": 1 - half}
+    slot_count = levels + 1
+    per_panel = x_ref.shape[0] // block
+    steps = act.shape[1] // block
+    loads = []
+    for k, (src, dst) in enumerate(((wu_any, wu), (vu_any, vu), (wd_any, wd), (vd_any, vd))):
+        loads.append(pltpu.make_async_copy(src, dst, lsem.at[k]))
+        loads[-1].start()
+    meet(n, me, half)
+
+    def to_partner(src, dst, kind, level):
+        return remote(
+            src,
+            dst,
+            psend.at[kind, level],
+            precv.at[kind, level],
+            {"tensor": flip(me, 1 << level)},
+        )
+
+    twins = []
+
+    def to_twin(src, dst):
+        k = len(twins)
+        twins.append(remote(src, dst, dsend.at[k], drecv.at[k], twin))
+
+    def halves_to_twin(rows_ref, dst):
+        rows = block // 2
+        for b in range(per_panel):
+            at = pl.ds(pl.multiple_of(b * block + (1 - half) * rows, rows), rows)
+            to_twin(rows_ref.at[:, at, :], dst.at[:, b])
+
+    def turn(panels, turned, slot):
+        for b in range(per_panel):
+            turned[slot, b] = panels[slot, b * block : (b + 1) * block, :].T
+
+    order = tuple(reversed(range(levels)))
+    xs = {level: to_partner(x_ref, xg.at[level + 1], 0, level) for level in order}
+    to_twin(x_ref, xown_p)
+    to_twin(c_ref, cown_p)
+    part, slots, pair, send, recv = first
+    part[0] = tn(x_ref[...], uu[...])
+    part[1] = tn(c_ref[...], ud[...])
+    sums = scatter_sums(n, me, part, slots, send, recv)
+    xg[0] = x_ref[...]
+    cg[0] = c_ref[...]
+    turn(xg, xt, 0)
+    turn(cg, ct, 0)
+    acc[...] = jnp.zeros_like(acc)
+    second[0][...] = jnp.zeros_like(second[0])
+    third[0][...] = jnp.zeros_like(third[0])
+    crossing = cross_sums(n, me, part, slots, pair, send, recv, sums)
+    rows = gather_sums(n, me, pair, lowf, send, recv, crossing)
+    cs = {}
+    for level in range(levels):
+        xs[level].wait()
+        cs[level] = to_partner(c_ref, cg.at[level + 1], 1, level)
+        turn(xg, xt, level + 1)
+    halves_to_twin(xg, x_p)
+    for copy in rows:
+        copy.wait()
+    to_twin(lowf, lowf_p)
+    for load in loads:
+        load.wait()
+
+    def add_blocks(kind, table, step, weights, hidden):
+        cols = pl.ds(pl.multiple_of(step * block, block), block)
+        for slot in range(slot_count):
+            term = nt(weights[slot, :, cols], hidden)
+            for b in range(per_panel):
+                here = (tables[table, slot, step] == b).astype(F32)
+                acc[slot, kind, b] += term * here
+
+    def forward(step, carry):
+        cols = pl.ds(pl.multiple_of(step * block, block), block)
+        values = nt(lowf[0], vu[cols, :])
+        for slot in range(slot_count):
+            values = values + nn(xt[slot, tables[0, slot, step]], wu[slot, :, cols])
+        cdf = 0.5 * (1.0 + lax.erf(values * root_half))
+        slope[:, cols] = cdf + values * jnp.exp(-0.5 * values * values) * inv_root_tau
+        hidden = (values * cdf).astype(BF16)
+        act[:, cols] = hidden
+        second[0][0] += nn(hidden, vd[cols, :])
+        add_blocks(0, 1, step, wd, hidden)
+        return carry
+
+    def backward(step, carry):
+        cols = pl.ds(pl.multiple_of(step * block, block), block)
+        values = nt(lowf[1], vd[cols, :])
+        for slot in range(slot_count):
+            values = values + nn(ct[slot, tables[1, slot, step]], wd[slot, :, cols])
+        hidden = (values * slope[:, cols]).astype(BF16)
+        pre[:, cols] = hidden
+        third[0][0] += nn(hidden, vu[cols, :])
+        add_blocks(1, 0, step, wu, hidden)
+        return carry
+
+    def hand_on(kind):
+        copies = []
+        for level in order:
+            for b in range(per_panel):
+                at = slice(b * block, (b + 1) * block)
+                away[level, kind, at, :] = acc[level + 1, kind, b].astype(BF16)
+            copies.append(to_partner(away.at[level, kind], home.at[level, kind], 2 + kind, level))
+        for b in range(per_panel):
+            own[kind, b * block : (b + 1) * block, :] = acc[0, kind, b]
+        return copies
+
+    lax.fori_loop(0, steps, forward, 0)
+    part_a, slots_a, pair_a, send_a, recv_a = second
+    sums_a = scatter_sums(n, me, part_a, slots_a, send_a, recv_a)
+    partials = hand_on(0)
+    to_twin(act, act_p)
+    for level in cs:
+        cs[level].wait()
+        turn(cg, ct, level + 1)
+    halves_to_twin(cg, c_p)
+    crossing_a = cross_sums(n, me, part_a, slots_a, pair_a, send_a, recv_a, sums_a)
+    lax.fori_loop(0, steps, backward, 0)
+    part_b, slots_b, pair_b, send_b, recv_b = third
+    sums_b = scatter_sums(n, me, part_b, slots_b, send_b, recv_b)
+    partials = partials + hand_on(1)
+    to_twin(pre, pre_p)
+    rows_a = gather_sums(n, me, pair_a, low_a, send_a, recv_a, crossing_a)
+    crossing_b = cross_sums(n, me, part_b, slots_b, pair_b, send_b, recv_b, sums_b)
+    rows_b = gather_sums(n, me, pair_b, low_b, send_b, recv_b, crossing_b)
+    for copy in rows_a:
+        copy.wait()
+    to_twin(low_a, lowa_p)
+    for copy in rows_b:
+        copy.wait()
+    to_twin(low_b, lowb_p)
+    for copy in partials + twins:
+        copy.wait()
+
+
+def layer(tables, features, cotangent, u_up, u_down, w_up, w_down, v_up, v_down, n):
+    slot_count, block, hidden = w_up.shape
+    levels = slot_count - 1
+    dim, tokens = features.shape
+    rank = u_up.shape[1]
+    per_panel = dim // block
+    vmem = pl.BlockSpec(memory_space=pltpu.VMEM)
+    far = pl.BlockSpec(memory_space=pl.ANY)
+    b16 = lambda *s: jax.ShapeDtypeStruct(s, BF16)
+    copies = 7 + 2 * per_panel
+    return pl.pallas_call(
+        functools.partial(layer_kernel, n, levels, block),
+        out_shape=(
+            b16(slot_count, dim, tokens),
+            b16(slot_count, dim, tokens),
+            b16(2, tokens, rank),
+            b16(tokens, hidden),
+            b16(tokens, hidden),
+            jax.ShapeDtypeStruct((2, dim, tokens), F32),
+            b16(levels, 2, dim, tokens),
+            b16(1, tokens, rank),
+            b16(1, tokens, rank),
+            b16(tokens, hidden),
+            b16(tokens, hidden),
+            b16(slot_count, per_panel, block // 2, tokens),
+            b16(slot_count, per_panel, block // 2, tokens),
+            b16(dim, tokens),
+            b16(dim, tokens),
+            b16(2, tokens, rank),
+            b16(1, tokens, rank),
+            b16(1, tokens, rank),
+        ),
+        in_specs=[pl.BlockSpec(memory_space=pltpu.SMEM)] + [vmem] * 4 + [far] * 4,
+        out_specs=(vmem,) * 18,
+        scratch_shapes=[
+            *sum_scratch(n, 2, tokens, rank),
+            *sum_scratch(n, 1, tokens, rank),
+            *sum_scratch(n, 1, tokens, rank),
+            pltpu.VMEM(w_up.shape, BF16),
+            pltpu.VMEM(w_down.shape, BF16),
+            pltpu.VMEM(v_up.shape, BF16),
+            pltpu.VMEM(v_down.shape, BF16),
+            pltpu.VMEM((slot_count, per_panel, tokens, block), BF16),
+            pltpu.VMEM((slot_count, per_panel, tokens, block), BF16),
+            pltpu.VMEM((tokens, hidden), F32),
+            pltpu.VMEM((slot_count, 2, per_panel, block, tokens), F32),
+            pltpu.VMEM((levels, 2, dim, tokens), BF16),
+            pltpu.SemaphoreType.DMA((4,)),
+            pltpu.SemaphoreType.DMA((4, levels)),
+            pltpu.SemaphoreType.DMA((4, levels)),
+            pltpu.SemaphoreType.DMA((copies,)),
+            pltpu.SemaphoreType.DMA((copies,)),
+        ],
+        compiler_params=pltpu.CompilerParams(
+            collective_id=0, has_side_effects=True, vmem_limit_bytes=VMEM_BYTES
+        ),
+    )(tables, features, cotangent, u_up, u_down, w_up, w_down, v_up, v_down)
+
+
+def final_kernel(
+    slot_count,
+    block,
+    tables,
+    xg,
+    cg,
+    x_p,
+    c_p,
+    xown_p,
+    cown_p,
+    lowf,
+    low_a,
+    low_b,
+    lowf_p,
+    lowa_p,
+    lowb_p,
+    own,
+    home,
+    uu,
+    ud,
+    act,
+    pre,
+    act_p,
+    pre_p,
+    out,
+    gfeat,
+    gwu,
+    gwd,
+    guu,
+    gvu,
+    gud,
+    gvd,
+):
+    step = pl.program_id(0)
+    half = tables[2, 0, 0]
+    rows = block // 2
+    width = lowf.shape[2] // 2
+    cols = pl.ds(pl.multiple_of(half * width, width), width)
+    for slot in range(slot_count):
+        for table, mine, twin, hid, hid_p, grad in (
+            (0, xg, x_p, pre, pre_p, gwu),
+            (1, cg, c_p, act, act_p, gwd),
+        ):
+            b = tables[table, slot, step]
+            at = pl.ds(pl.multiple_of(b * block + half * rows, rows), rows)
+            grad[slot] = nn(mine[slot, at, :], hid[...]) + nn(twin[slot, b], hid_p[...])
+    gvu[...] = tn(pre[...], lowf[0, :, cols]) + tn(pre_p[...], lowf_p[0, :, cols])
+    gvd[...] = tn(act[...], lowf[1, :, cols]) + tn(act_p[...], lowf_p[1, :, cols])
+
+    @pl.when(step == 0)
+    def _():
+        for kind, u, low, result in ((0, ud, low_a, out), (1, uu, low_b, gfeat)):
+            total = own[kind] + nt(u[...], low[0])
+            for level in range(slot_count - 1):
+                total = total + home[level, kind].astype(F32)
+            result[...] = total.astype(BF16)
+        guu[...] = nn(xg[0], low_b[0, :, cols]) + nn(xown_p[...], lowb_p[0, :, cols])
+        gud[...] = nn(cg[0], low_a[0, :, cols]) + nn(cown_p[...], lowa_p[0, :, cols])
+
+
+def finish(tables, xg, cg, x_p, c_p, xown_p, cown_p, lowf, low_a, low_b, lowf_p, lowa_p, lowb_p, own, home, u_up, u_down,
+           act, pre, act_p, pre_p, block):
+    slot_count, dim, tokens = xg.shape
+    hidden = act.shape[1]
+    rank = lowf.shape[2]
+    full = lambda a: pl.BlockSpec(a.shape, lambda c, *_: (0,) * a.ndim)
+    hid = pl.BlockSpec((tokens, block), lambda c, *_: (0, c))
+    gw = pl.BlockSpec((slot_count, block // 2, block), lambda c, *_: (0, 0, c))
+    gv = pl.BlockSpec((block, rank // 2), lambda c, *_: (c, 0))
+    once = lambda *shape: pl.BlockSpec(shape, lambda c, *_: (0,) * len(shape))
+    fixed = (xg, cg, x_p, c_p, xown_p, cown_p, lowf, low_a, low_b, lowf_p, lowa_p, lowb_p, own, home, u_up, u_down)
+    return pl.pallas_call(
+        functools.partial(final_kernel, slot_count, block),
+        out_shape=(
+            jax.ShapeDtypeStruct((dim, tokens), BF16),
+            jax.ShapeDtypeStruct((dim, tokens), BF16),
+            jax.ShapeDtypeStruct((slot_count, block // 2, hidden), F32),
+            jax.ShapeDtypeStruct((slot_count, block // 2, hidden), F32),
+            jax.ShapeDtypeStruct((dim, rank // 2), F32),
+            jax.ShapeDtypeStruct((hidden, rank // 2), F32),
+            jax.ShapeDtypeStruct((dim, rank // 2), F32),
+            jax.ShapeDtypeStruct((hidden, rank // 2), F32),
+        ),
+        grid_spec=pltpu.PrefetchScalarGridSpec(
+            num_scalar_prefetch=1,
+            grid=(hidden // block,),
+            in_specs=[full(a) for a in fixed] + [hid] * 4,
+            out_specs=(
+                once(dim, tokens),
+                once(dim, tokens),
+                gw,
+                gw,
+                once(dim, rank // 2),
+                gv,
+                once(dim, rank // 2),
+                gv,
+            ),
+        ),
+        compiler_params=pltpu.CompilerParams(vmem_limit_bytes=VMEM_BYTES),
+    )(tables, *fixed, act, pre, act_p, pre_p)
+
+
+def one_panel_each(
+    features, table_up, table_down, w_up, u_up, v_up, w_down, u_down, v_down, cotangent
+):
+    slot_count, block, hidden = w_up.shape
+    levels = slot_count - 1
+    n = lax.axis_size("tensor")
+    me = lax.axis_index("tensor")
+    count = hidden // block
+    tables = lax.dynamic_slice_in_dim(jnp.stack([table_up, table_down]), me * count, count, 2)
+    half = jnp.full((1,) + tables.shape[1:], lax.axis_index("dp"), jnp.int32)
+    tables = jnp.concatenate([tables, half])
+    (xg, cg, lowf, act, pre, own, home, low_a, low_b, act_p, pre_p, x_p, c_p, xown_p, cown_p, lowf_p,
+     lowa_p, lowb_p) = layer(
+        tables, features, cotangent, u_up, u_down, w_up, w_down, v_up, v_down, n
+    )
+    return finish(tables, xg, cg, x_p, c_p, xown_p, cown_p, lowf, low_a, low_b, lowf_p, lowa_p, lowb_p,
+                  own, home, u_up, u_down, act, pre, act_p, pre_p, block)
+
+
+def solve(*args):
+    slot_count = args[3].shape[0]
+    fits = (
+        slot_count > 1
+        and lax.axis_size("tensor") == 1 << slot_count - 1
+        and lax.axis_size("dp") == 2
+        and args[3].shape[2] % args[3].shape[1] == 0
+    )
+    return one_panel_each(*args) if fits else on_device(*args)
+
+
 def solution(mesh):
     return jax.shard_map(
-        on_device,
+        solve,
         mesh=mesh,
         in_specs=(
             P("tensor", ("groups", "dp")),

time: 476 us -> 110 us (0.23); the launches traced: 467 us -> 110 us
  waiting for transfers between devices: 146 us -> 0 us
  blocking collectives: 126 us -> 0 us
  Pallas kernels: 0 us -> 108 us
  local copies, waits for them, and re-layouts: 101 us -> 0.6 us
  matrix products: 47.6 us -> 0 us
  other arithmetic: 16.4 us -> 0.78 us
  between operations: 15.1 us -> 0.65 us
  starting transfers between devices: 14.3 us -> 0 us
    ppermute x12 -> x0, waiting for transfers between devices: 146 us -> none  [from_partner(): lax.ppermute(array, axis, [(i, i ^ 1 << distance) for i in range(lax.axis...]
    psum x2 -> x0, blocking collectives: 126 us -> none  [the longest x1 86.1 us: on_device(): lax.psum(jnp.dot(u_up.T, features, preferred_element_type=jnp.float32), '...]
    pallas_call x0 -> x2, Pallas kernels: none -> 108 us  [the longest x1 93.4 us: layer(): pl.pallas_call(functools.partial(layer_kernel, n, levels, block), out_sha...]
    dot_general x26 -> x0, matrix products: 47.6 us -> none  [the longest x8 11.8 us: place_blocks(): jnp.einsum('bn,brt->nrt', onehot, portion, precision=lax.Precision.HIGHEST)]
    unnamed x89 -> x0, local copies, waits for them, and re-layouts: 29.3 us -> none
    ppermute x6 -> x0, local copies, waits for them, and re-layouts: 16.7 us -> none  [from_partner(): lax.ppermute(array, axis, [(i, i ^ 1 << distance) for i in range(lax.axis...]
    reshape x5 -> x0, local copies, waits for them, and re-layouts: 16.5 us -> none  [the longest x1 7.45 us: on_device(): w_down.reshape(slot_count, block_rows, block_count, column_width)]
    gather x16 -> x0, local copies, waits for them, and re-layouts: 15.9 us -> none  [the longest x8 10.7 us: pick_blocks(): return jnp.take(stacked, chosen, axis=0)]
  transfers between devices with their start and end apart: 18 -> 0, of which waited for: 4 -> 0; matrix products, arithmetic and copies ran while one was open for 30% -> 0% of each run, Pallas kernels for 0% -> 0%
where the time goes in v3:
time: 110 us
  Pallas kernels  108 us (98%)
    pallas_call x1, Pallas kernels, layer(): pl.pallas_call(functools.partial(layer_kernel, n, levels, block), out_sha...  93.4 us
    pallas_call x1, Pallas kernels, finish(): pl.pallas_call(functools.partial(final_kernel, slot_count, block), out_sh...  14.7 us

profile of v3, /device:TPU:0, one launch (start us, length us, event | category | flops | bytes accessed | tf_op | source)
XLA Modules:
  0.0 110.1 jit_solution(11865883693666551698)
XLA Ops:
  0.6 0.8 dynamic-slice_add_fusion
  1.4 0.6 concatenate.3.tables
  2.0 93.4 %shard_map.161 = (bf16[4,512,256]{2,1,0:T(8,128)(2,1)}, bf16[4,512,256]{2,1,0:T(8,128)(2,1)}, bf16[2,256,256]{2,1,0:T(8,128)(2,1)}, bf16[256,2048]{1,0:T(8,128)(...) custom-call(s32[3,4,8]{2,1,0:T(4,128)} %concatenate.3.tables, ...), custom_call_target="tpu_custom_call" | custom-call | tf_op jit(solution)/shard_map/pallas_call | solution.py:477
  95.5 14.7 %shard_map.162 = (bf16[512,256]{1,0:T(8,128)(2,1)}, bf16[512,256]{1,0:T(8,128)(2,1)}, f32[4,128,2048]{2,1,0:T(8,128)}, f32[4,128,2048]{2,1,0:T(8,128)}, f32[512,...) custom-call(s32[3,4,8]{2,1,0:T(4,128)} %concatenate.3.tables, ...), custom_call_target="tpu_custom_call" | custom-call | tf_op jit(solution)/shard_map/pallas_call | solution.py:597

commit v4 on v3

--- a/solution.py
+++ b/solution.py
@@ -322,7 +322,7 @@
     ]
 
 
-def layer_kernel(n, levels, block, tables, x_ref, c_ref, uu, ud, wu_any, wd_any, vu_any, vd_any, *refs):
+def layer_kernel(n, levels, block, table_up, table_down, x_ref, c_ref, uu, ud, wu_any, wd_any, vu_any, vd_any, *refs):
     (xg, cg, lowf, act, pre, own, home, low_a, low_b, act_p, pre_p, x_p, c_p) = refs[:13]
     (xown_p, cown_p, lowf_p, lowa_p, lowb_p) = refs[13:18]
     first, second, third = refs[18:23], refs[23:28], refs[28:33]
@@ -333,6 +333,8 @@
     slot_count = levels + 1
     per_panel = x_ref.shape[0] // block
     steps = act.shape[1] // block
+    tables = (table_up, table_down)
+    base = me * steps
     loads = []
     for k, (src, dst) in enumerate(((wu_any, wu), (vu_any, vu), (wd_any, wd), (vd_any, vd))):
         loads.append(pltpu.make_async_copy(src, dst, lsem.at[k]))
@@ -393,45 +395,48 @@
     for load in loads:
         load.wait()
 
-    def add_blocks(kind, table, step, weights, hidden):
-        cols = pl.ds(pl.multiple_of(step * block, block), block)
-        for slot in range(slot_count):
-            term = nt(weights[slot, :, cols], hidden)
+    def add_slot(kind, slot, weights, hidden):
+        def add(step, carry):
+            cols = pl.ds(pl.multiple_of(step * block, block), block)
+            term = nt(weights[slot, :, cols], hidden[:, cols])
             for b in range(per_panel):
-                here = (tables[table, slot, step] == b).astype(F32)
+                here = (tables[1 - kind][slot, base + step] == b).astype(F32)
                 acc[slot, kind, b] += term * here
+            return carry
+
+        lax.fori_loop(0, steps, add, 0)
 
     def forward(step, carry):
         cols = pl.ds(pl.multiple_of(step * block, block), block)
         values = nt(lowf[0], vu[cols, :])
         for slot in range(slot_count):
-            values = values + nn(xt[slot, tables[0, slot, step]], wu[slot, :, cols])
+            values = values + nn(xt[slot, tables[0][slot, base + step]], wu[slot, :, cols])
         cdf = 0.5 * (1.0 + lax.erf(values * root_half))
         slope[:, cols] = cdf + values * jnp.exp(-0.5 * values * values) * inv_root_tau
         hidden = (values * cdf).astype(BF16)
         act[:, cols] = hidden
         second[0][0] += nn(hidden, vd[cols, :])
-        add_blocks(0, 1, step, wd, hidden)
         return carry
 
     def backward(step, carry):
         cols = pl.ds(pl.multiple_of(step * block, block), block)
         values = nt(lowf[1], vd[cols, :])
         for slot in range(slot_count):
-            values = values + nn(ct[slot, tables[1, slot, step]], wd[slot, :, cols])
+            values = values + nn(ct[slot, tables[1][slot, base + step]], wd[slot, :, cols])
         hidden = (values * slope[:, cols]).astype(BF16)
         pre[:, cols] = hidden
         third[0][0] += nn(hidden, vu[cols, :])
-        add_blocks(1, 0, step, wu, hidden)
         return carry
 
-    def hand_on(kind):
+    def hand_on(kind, weights, hidden):
         copies = []
         for level in order:
+            add_slot(kind, level + 1, weights, hidden)
             for b in range(per_panel):
                 at = slice(b * block, (b + 1) * block)
                 away[level, kind, at, :] = acc[level + 1, kind, b].astype(BF16)
             copies.append(to_partner(away.at[level, kind], home.at[level, kind], 2 + kind, level))
+        add_slot(kind, 0, weights, hidden)
         for b in range(per_panel):
             own[kind, b * block : (b + 1) * block, :] = acc[0, kind, b]
         return copies
@@ -439,8 +444,8 @@
     lax.fori_loop(0, steps, forward, 0)
     part_a, slots_a, pair_a, send_a, recv_a = second
     sums_a = scatter_sums(n, me, part_a, slots_a, send_a, recv_a)
-    partials = hand_on(0)
     to_twin(act, act_p)
+    partials = hand_on(0, wd, act)
     for level in cs:
         cs[level].wait()
         turn(cg, ct, level + 1)
@@ -449,8 +454,8 @@
     lax.fori_loop(0, steps, backward, 0)
     part_b, slots_b, pair_b, send_b, recv_b = third
     sums_b = scatter_sums(n, me, part_b, slots_b, send_b, recv_b)
-    partials = partials + hand_on(1)
     to_twin(pre, pre_p)
+    partials = partials + hand_on(1, wu, pre)
     rows_a = gather_sums(n, me, pair_a, low_a, send_a, recv_a, crossing_a)
     crossing_b = cross_sums(n, me, part_b, slots_b, pair_b, send_b, recv_b, sums_b)
     rows_b = gather_sums(n, me, pair_b, low_b, send_b, recv_b, crossing_b)
@@ -464,7 +469,7 @@
         copy.wait()
 
 
-def layer(tables, features, cotangent, u_up, u_down, w_up, w_down, v_up, v_down, n):
+def layer(table_up, table_down, features, cotangent, u_up, u_down, w_up, w_down, v_up, v_down, n):
     slot_count, block, hidden = w_up.shape
     levels = slot_count - 1
     dim, tokens = features.shape
@@ -496,7 +501,7 @@
             b16(1, tokens, rank),
             b16(1, tokens, rank),
         ),
-        in_specs=[pl.BlockSpec(memory_space=pltpu.SMEM)] + [vmem] * 4 + [far] * 4,
+        in_specs=[pl.BlockSpec(memory_space=pltpu.SMEM)] * 2 + [vmem] * 4 + [far] * 4,
         out_specs=(vmem,) * 18,
         scratch_shapes=[
             *sum_scratch(n, 2, tokens, rank),
@@ -520,13 +525,14 @@
         compiler_params=pltpu.CompilerParams(
             collective_id=0, has_side_effects=True, vmem_limit_bytes=VMEM_BYTES
         ),
-    )(tables, features, cotangent, u_up, u_down, w_up, w_down, v_up, v_down)
+    )(table_up, table_down, features, cotangent, u_up, u_down, w_up, w_down, v_up, v_down)
 
 
 def final_kernel(
     slot_count,
     block,
-    tables,
+    table_up,
+    table_down,
     xg,
     cg,
     x_p,
@@ -557,18 +563,23 @@
     gvd,
 ):
     step = pl.program_id(0)
-    half = tables[2, 0, 0]
+    half = lax.axis_index("dp")
+    base = lax.axis_index("tensor") * pl.num_programs(0)
     rows = block // 2
     width = lowf.shape[2] // 2
     cols = pl.ds(pl.multiple_of(half * width, width), width)
-    for slot in range(slot_count):
-        for table, mine, twin, hid, hid_p, grad in (
-            (0, xg, x_p, pre, pre_p, gwu),
-            (1, cg, c_p, act, act_p, gwd),
-        ):
-            b = tables[table, slot, step]
+    for table, mine, twin, hid, hid_p, grad in (
+        (table_up, xg, x_p, pre, pre_p, gwu),
+        (table_down, cg, c_p, act, act_p, gwd),
+    ):
+        ours, theirs = [], []
+        for slot in range(slot_count):
+            b = table[slot, base + step]
             at = pl.ds(pl.multiple_of(b * block + half * rows, rows), rows)
-            grad[slot] = nn(mine[slot, at, :], hid[...]) + nn(twin[slot, b], hid_p[...])
+            ours.append(mine[slot, at, :])
+            theirs.append(twin[slot, b])
+        total = nn(jnp.concatenate(ours), hid[...]) + nn(jnp.concatenate(theirs), hid_p[...])
+        grad[...] = total.reshape(grad.shape)
     gvu[...] = tn(pre[...], lowf[0, :, cols]) + tn(pre_p[...], lowf_p[0, :, cols])
     gvd[...] = tn(act[...], lowf[1, :, cols]) + tn(act_p[...], lowf_p[1, :, cols])
 
@@ -583,7 +594,7 @@
         gud[...] = nn(cg[0], low_a[0, :, cols]) + nn(cown_p[...], lowa_p[0, :, cols])
 
 
-def finish(tables, xg, cg, x_p, c_p, xown_p, cown_p, lowf, low_a, low_b, lowf_p, lowa_p, lowb_p, own, home, u_up, u_down,
+def finish(table_up, table_down, xg, cg, x_p, c_p, xown_p, cown_p, lowf, low_a, low_b, lowf_p, lowa_p, lowb_p, own, home, u_up, u_down,
            act, pre, act_p, pre_p, block):
     slot_count, dim, tokens = xg.shape
     hidden = act.shape[1]
@@ -607,7 +618,7 @@
             jax.ShapeDtypeStruct((hidden, rank // 2), F32),
         ),
         grid_spec=pltpu.PrefetchScalarGridSpec(
-            num_scalar_prefetch=1,
+            num_scalar_prefetch=2,
             grid=(hidden // block,),
             in_specs=[full(a) for a in fixed] + [hid] * 4,
             out_specs=(
@@ -622,7 +633,7 @@
             ),
         ),
         compiler_params=pltpu.CompilerParams(vmem_limit_bytes=VMEM_BYTES),
-    )(tables, *fixed, act, pre, act_p, pre_p)
+    )(table_up, table_down, *fixed, act, pre, act_p, pre_p)
 
 
 def one_panel_each(
@@ -631,16 +642,11 @@
     slot_count, block, hidden = w_up.shape
     levels = slot_count - 1
     n = lax.axis_size("tensor")
-    me = lax.axis_index("tensor")
-    count = hidden // block
-    tables = lax.dynamic_slice_in_dim(jnp.stack([table_up, table_down]), me * count, count, 2)
-    half = jnp.full((1,) + tables.shape[1:], lax.axis_index("dp"), jnp.int32)
-    tables = jnp.concatenate([tables, half])
     (xg, cg, lowf, act, pre, own, home, low_a, low_b, act_p, pre_p, x_p, c_p, xown_p, cown_p, lowf_p,
      lowa_p, lowb_p) = layer(
-        tables, features, cotangent, u_up, u_down, w_up, w_down, v_up, v_down, n
-    )
-    return finish(tables, xg, cg, x_p, c_p, xown_p, cown_p, lowf, low_a, low_b, lowf_p, lowa_p, lowb_p,
+        table_up, table_down, features, cotangent, u_up, u_down, w_up, w_down, v_up, v_down, n
+    )
+    return finish(table_up, table_down, xg, cg, x_p, c_p, xown_p, cown_p, lowf, low_a, low_b, lowf_p, lowa_p, lowb_p,
                   own, home, u_up, u_down, act, pre, act_p, pre_p, block)
 
 

time: 110 us -> 107 us (0.973)
  Pallas kernels: 108 us -> 106 us
    pallas_call x1, Pallas kernels: 93.4 us -> 91.8 us  [layer(): pl.pallas_call(functools.partial(layer_kernel, n, levels, block), out_sha...]
where the time goes in v4:
time: 107 us
  Pallas kernels  106 us (99%)
    pallas_call x1, Pallas kernels, layer(): pl.pallas_call(functools.partial(layer_kernel, n, levels, block), out_sha...  91.8 us
    pallas_call x1, Pallas kernels, finish(): pl.pallas_call(functools.partial(final_kernel, slot_count, block), out_sh...  14.6 us

profile of v4, /device:TPU:0, one launch (start us, length us, event | category | flops | bytes accessed | tf_op | source)
XLA Modules:
  0.0 107.1 jit_solution(17519286138342932132)
XLA Ops:
  0.6 91.8 %shard_map.161 = (bf16[4,512,256]{2,1,0:T(8,128)(2,1)}, bf16[4,512,256]{2,1,0:T(8,128)(2,1)}, bf16[2,256,256]{2,1,0:T(8,128)(2,1)}, bf16[256,2048]{1,0:T(8,128)(...) custom-call(s32[4,64]{1,0:T(4,128)} %table_up.3, ...), custom_call_target="tpu_custom_call" | custom-call | tf_op jit(solution)/shard_map/pallas_call | solution.py:482
  92.5 14.6 %shard_map.162 = (bf16[512,256]{1,0:T(8,128)(2,1)}, bf16[512,256]{1,0:T(8,128)(2,1)}, f32[4,128,2048]{2,1,0:T(8,128)}, f32[4,128,2048]{2,1,0:T(8,128)}, f32[512,...) custom-call(s32[4,64]{1,0:T(4,128)} %table_up.3, s32[4,64]{1,0:T(4,128)} %table_down.3, ...), custom_call_target="tpu_custom_call" | custom-call | tf_op jit(solution)/shard_map/pallas_call | solution.py:608

commit v5 on v4

--- a/solution.py
+++ b/solution.py
@@ -382,11 +382,10 @@
     second[0][...] = jnp.zeros_like(second[0])
     third[0][...] = jnp.zeros_like(third[0])
     crossing = cross_sums(n, me, part, slots, pair, send, recv, sums)
+    cs = {level: to_partner(c_ref, cg.at[level + 1], 1, level) for level in order}
     rows = gather_sums(n, me, pair, lowf, send, recv, crossing)
-    cs = {}
     for level in range(levels):
         xs[level].wait()
-        cs[level] = to_partner(c_ref, cg.at[level + 1], 1, level)
         turn(xg, xt, level + 1)
     halves_to_twin(xg, x_p)
     for copy in rows:
@@ -446,7 +445,7 @@
     sums_a = scatter_sums(n, me, part_a, slots_a, send_a, recv_a)
     to_twin(act, act_p)
     partials = hand_on(0, wd, act)
-    for level in cs:
+    for level in range(levels):
         cs[level].wait()
         turn(cg, ct, level + 1)
     halves_to_twin(cg, c_p)

time: 107 us -> 112 us (1.047)
  Pallas kernels: 106 us -> 111 us
    pallas_call x1, Pallas kernels: 91.8 us -> 96.2 us  [layer(): pl.pallas_call(functools.partial(layer_kernel, n, levels, block), out_sha...]
where the time goes in v5:
time: 112 us; the launch traced here: 111 us
  Pallas kernels  111 us (99%)
    pallas_call x1, Pallas kernels, layer(): pl.pallas_call(functools.partial(layer_kernel, n, levels, block), out_sha...  96.2 us
    pallas_call x1, Pallas kernels, finish(): pl.pallas_call(functools.partial(final_kernel, slot_count, block), out_sh...  14.6 us

profile of v5, /device:TPU:0, one launch (start us, length us, event | category | flops | bytes accessed | tf_op | source)
XLA Modules:
  0.0 111.4 jit_solution(2214563988938973940)
XLA Ops:
  0.6 96.2 %shard_map.161 = (bf16[4,512,256]{2,1,0:T(8,128)(2,1)}, bf16[4,512,256]{2,1,0:T(8,128)(2,1)}, bf16[2,256,256]{2,1,0:T(8,128)(2,1)}, bf16[256,2048]{1,0:T(8,128)(...) custom-call(s32[4,64]{1,0:T(4,128)} %table_up.3, ...), custom_call_target="tpu_custom_call" | custom-call | tf_op jit(solution)/shard_map/pallas_call | solution.py:481
  96.8 14.6 %shard_map.162 = (bf16[512,256]{1,0:T(8,128)(2,1)}, bf16[512,256]{1,0:T(8,128)(2,1)}, f32[4,128,2048]{2,1,0:T(8,128)}, f32[4,128,2048]{2,1,0:T(8,128)}, f32[512,...) custom-call(s32[4,64]{1,0:T(4,128)} %table_up.3, s32[4,64]{1,0:T(4,128)} %table_down.3, ...), custom_call_target="tpu_custom_call" | custom-call | tf_op jit(solution)/shard_map/pallas_call | solution.py:607
